TPU v7x, 32 devices: a whole 2x2x4 slice. The times are simulated.
32 devices in a mesh: dp: 8 (over y, x, core), mp: 4 (over z).
Axes of the slice: x: 2, y: 2, z: 4, core: 2. Of those that a mesh axis runs over, the one named last changes fastest.
Arguments:
- block_in: bfloat16 [8192, 1024], P('dp', 'mp'), may hold values from -6 to 6
- segments: int32 [8, 1024], P('dp'), may hold values from 0 to 3, never falling along the last dimension, each value on 1 to 800 neighbouring positions
- routes: int32 [8192, 8], P(('dp', 'mp')), may hold values from 0 to 31, all different within a row; in each aligned block of 256 rows (0 to 255, 256 to 511, ...) at most 96 rows name the same one
- attn_gain: float32 [1024], replicated, may hold values from 0.5 to 1.5
- w_query: bfloat16 [1024, 1024], P('dp', 'mp'), may hold values from -0.1875 to 0.1875
- w_key: bfloat16 [1024, 512], P('dp', 'mp'), may hold values from -0.1875 to 0.1875
- w_value: bfloat16 [1024, 512], P('dp', 'mp'), may hold values from -0.1875 to 0.1875
- w_out: bfloat16 [1024, 1024], P('dp', 'mp'), may hold values from -1.5 to 1.5
- moe_gain: float32 [1024], replicated, may hold values from 0.5 to 1.5
- w_router: bfloat16 [1024, 32], replicated, may hold values from -0.09375 to 0.09375
- w_gate_up: bfloat16 [32, 1024, 1024], P('dp', None, 'mp'), may hold values from -0.1875 to 0.1875
- w_down: bfloat16 [32, 512, 1024], P('dp', None, 'mp'), may hold values from -1 to 1
- grad_out: bfloat16 [8192, 1024], P(('dp', 'mp')), may hold values from -6 to 6
Outputs:
- block_out: bfloat16 [8192, 1024], P(('dp', 'mp'))
- grad_in: float32 [8192, 1024], P(('dp', 'mp'))
- grad_attn_gain: float32 [1024], replicated
- grad_w_query: float32 [1024, 1024], P('dp', 'mp')
- grad_w_key: float32 [1024, 512], P('dp', 'mp')
- grad_w_value: float32 [1024, 512], P('dp', 'mp')
- grad_w_out: float32 [1024, 1024], P('dp', 'mp')
- grad_moe_gain: float32 [1024], replicated
- grad_w_router: float32 [1024, 32], replicated
- grad_w_gate_up: float32 [32, 1024, 1024], P('dp', None, 'mp')
- grad_w_down: float32 [32, 512, 1024], P('dp', None, 'mp')
Inputs may be any that keep to these rules, and one draw needn't show every extreme that they name: `routes`: each token names 8 different experts. Among the 256 rows of one device no expert is named more than 96 times, and some expert reaches 96 in some device's rows. `segments`: along each sequence the numbers never fall and start at 0; each document has 1 to 800 tokens, one exactly 800.
All inputs are finite; a program needn't handle non-finite values.
Results may differ from a plain program's by a relative error of at most 0.019.
Values may be sent and summed in bfloat16 or wider, within the bound.
A program may use at most 192 MiB of HBM per device.

v0:
```python
import math

import jax
import jax.numpy as jnp
from jax import lax
from jax.sharding import PartitionSpec as P

D = 1024
HD = 64
EXPERTS = 32
FF = 512
TOPK = 8
CAP = 96


EPS = 1e-06
ROPE_BASE = 10000.0
NEG_FILL = -1000000000.0
HIGH = lax.Precision.HIGHEST


def rms_scale(values, gain):
    return values * lax.rsqrt(jnp.mean(values * values, axis=-1, keepdims=True) + EPS) * gain


def positions_of(seg_row):
    index = jnp.arange(seg_row.shape[0], dtype=jnp.int32)
    change = jnp.concatenate([jnp.ones((1,), dtype=bool), seg_row[1:] != seg_row[:-1]])
    begin = lax.cummax(jnp.where(change, index, jnp.zeros_like(index)), axis=0)
    return index - begin


def angles(seg_row):
    place = positions_of(seg_row).astype(jnp.float32)
    freq = ROPE_BASE ** (-jnp.arange(0, HD, 2).astype(jnp.float32) / HD)
    theta = place[:, None] * freq[None, :]
    theta = jnp.concatenate([theta, theta], axis=1)
    return (jnp.cos(theta)[:, None, :], jnp.sin(theta)[:, None, :])


def rotate(values, cosine, sine):
    half = values.shape[-1] // 2
    turned = jnp.concatenate([-values[..., half:], values[..., :half]], axis=-1)
    return values * cosine + turned * sine


def unrotate(values, cosine, sine):
    half = values.shape[-1] // 2
    spun = values * sine
    return values * cosine + jnp.concatenate([spun[..., half:], -spun[..., :half]], axis=-1)


def allowed_pairs(seg_row):
    index = jnp.arange(seg_row.shape[0], dtype=jnp.int32)
    return (seg_row[:, None] == seg_row[None, :]) & (index[:, None] >= index[None, :])


def attend_forward(packed):
    query, key, value, seg_row = packed
    length = seg_row.shape[0]
    cosine, sine = angles(seg_row)
    query_rot = rotate(query, cosine, sine).astype(jnp.bfloat16)
    key_rot = rotate(key, cosine, sine).astype(jnp.bfloat16)
    value_low = value.astype(jnp.bfloat16)
    grouped = query_rot.reshape(length, key.shape[1], -1, HD)
    scores = jnp.einsum("qkgd,skd->kgqs", grouped, key_rot, preferred_element_type=jnp.float32) * (
        1.0 / math.sqrt(HD)
    )
    scores = jnp.where(allowed_pairs(seg_row), scores, NEG_FILL)
    top_score = jnp.max(scores, axis=-1, keepdims=True)
    expos = jnp.exp(scores - top_score)
    totals = jnp.sum(expos, axis=-1, keepdims=True)
    probs_low = (expos / totals).astype(jnp.bfloat16)
    mixed = jnp.einsum("kgqs,skd->qkgd", probs_low, value_low, preferred_element_type=jnp.float32)
    log_total = top_score + jnp.log(totals)
    return (
        mixed.reshape(length, -1).astype(jnp.bfloat16),
        log_total,
        query_rot,
        key_rot,
        value_low,
    )


def attend_backward(packed):
    grad_mixed, query_rot, key_rot, value_low, log_total, seg_row = packed
    length = seg_row.shape[0]
    kv_heads = key_rot.shape[1]
    scale = 1.0 / math.sqrt(HD)
    grouped = query_rot.reshape(length, kv_heads, -1, HD)
    scores = (
        jnp.einsum("qkgd,skd->kgqs", grouped, key_rot, preferred_element_type=jnp.float32) * scale
    )
    scores = jnp.where(allowed_pairs(seg_row), scores, NEG_FILL)
    probs = jnp.exp(scores - log_total)
    grad_grouped = grad_mixed.reshape(length, kv_heads, -1, HD)
    grad_value = jnp.einsum(
        "kgqs,qkgd->skd",
        probs.astype(jnp.bfloat16),
        grad_grouped,
        preferred_element_type=jnp.float32,
    )
    grad_probs = jnp.einsum(
        "qkgd,skd->kgqs", grad_grouped, value_low, preferred_element_type=jnp.float32
    )
    centre = jnp.sum(probs * grad_probs, axis=-1, keepdims=True)
    grad_scores = (probs * (grad_probs - centre)).astype(jnp.bfloat16)
    grad_query = (
        jnp.einsum("kgqs,skd->qkgd", grad_scores, key_rot, preferred_element_type=jnp.float32)
        * scale
    )
    grad_key = (
        jnp.einsum("kgqs,qkgd->skd", grad_scores, grouped, preferred_element_type=jnp.float32)
        * scale
    )
    cosine, sine = angles(seg_row)
    grad_query = unrotate(grad_query.reshape(length, -1, HD), cosine, sine)
    grad_key = unrotate(grad_key, cosine, sine)
    return (
        grad_query.reshape(length, -1).astype(jnp.bfloat16),
        grad_key.reshape(length, -1).astype(jnp.bfloat16),
        grad_value.reshape(length, -1).astype(jnp.bfloat16),
    )


def local(
    block_in,
    segments,
    routes,
    attn_gain,
    w_query,
    w_key,
    w_value,
    w_out,
    moe_gain,
    w_router,
    w_gate_up,
    w_down,
    grad_out,
):
    mp_index = lax.axis_index("mp")
    dp_size = lax.axis_size("dp")
    tok_dev = routes.shape[0]
    seqs_here = segments.shape[0]
    full_rows = lax.all_gather(block_in, "mp", axis=1, tiled=True)
    row_count = full_rows.shape[0]
    length = row_count // seqs_here
    wide = full_rows.astype(jnp.float32)
    normed_low = rms_scale(wide, attn_gain).astype(jnp.bfloat16)
    query_full, key_full, value_full, out_part = (
        lax.all_gather(w_query, "dp", axis=0, tiled=True),
        lax.all_gather(w_key, "dp", axis=0, tiled=True),
        lax.all_gather(w_value, "dp", axis=0, tiled=True),
        lax.all_gather(w_out, "dp", axis=0, tiled=True),
    )
    query = jnp.dot(normed_low, query_full, preferred_element_type=jnp.float32)
    key = jnp.dot(normed_low, key_full, preferred_element_type=jnp.float32)
    value = jnp.dot(normed_low, value_full, preferred_element_type=jnp.float32)
    head_local = query_full.shape[1] // HD
    kv_local = key_full.shape[1] // HD
    mixed, log_total, query_rot, key_rot, value_low = lax.map(
        attend_forward,
        (
            query.reshape(seqs_here, length, head_local, HD),
            key.reshape(seqs_here, length, kv_local, HD),
            value.reshape(seqs_here, length, kv_local, HD),
            segments,
        ),
    )
    heads_low = mixed.reshape(row_count, head_local * HD)
    row_start = mp_index * tok_dev
    attn_mixed = lax.psum_scatter(
        jnp.einsum("rh,dh->rd", heads_low, out_part, preferred_element_type=jnp.float32),
        "mp",
        scatter_dimension=0,
        tiled=True,
    )
    own_rows = lax.dynamic_slice_in_dim(wide, row_start, tok_dev, 0)
    hidden = own_rows + attn_mixed
    moe_low = rms_scale(hidden, moe_gain).astype(jnp.bfloat16)
    logits = jnp.dot(moe_low, w_router, preferred_element_type=jnp.float32)
    chosen = routes[:, :, None] == jnp.arange(EXPERTS, dtype=jnp.int32)[None, None, :]
    picked = jnp.sum(jnp.where(chosen, logits[:, None, :], 0.0), axis=2)
    gates = jax.nn.softmax(picked, axis=1)
    flat_routes = routes.reshape(-1)
    onehot = (flat_routes[:, None] == jnp.arange(EXPERTS, dtype=jnp.int32)[None, :]).astype(
        jnp.int32
    )
    rank = jnp.sum((jnp.cumsum(onehot, axis=0) - 1) * onehot, axis=1)
    slot = flat_routes * CAP + rank
    exp_dev = EXPERTS // dp_size
    send_rows = (
        jnp.zeros((EXPERTS * CAP, D), jnp.bfloat16).at[slot].set(jnp.repeat(moe_low, TOPK, axis=0))
    )
    arrived = lax.all_to_all(
        send_rows.reshape(dp_size, exp_dev * CAP, D), "dp", split_axis=0, concat_axis=0, tiled=True
    ).reshape(dp_size, exp_dev, CAP, D)
    gate_up, down_full = (
        lax.all_gather(w_gate_up, "mp", axis=2, tiled=True),
        lax.all_gather(w_down, "mp", axis=2, tiled=True),
    )
    both = jnp.einsum("secd,edf->secf", arrived, gate_up, preferred_element_type=jnp.float32)
    gate_part = both[..., :FF]
    up_part = both[..., FF:]
    act_low = (jax.nn.silu(gate_part) * up_part).astype(jnp.bfloat16)
    expert_out = jnp.einsum(
        "secf,efd->secd", act_low, down_full, preferred_element_type=jnp.float32
    ).astype(jnp.bfloat16)
    returned = lax.all_to_all(
        expert_out.reshape(dp_size, exp_dev * CAP, D), "dp", split_axis=0, concat_axis=0, tiled=True
    ).reshape(EXPERTS * CAP, D)
    picked_rows = returned[slot].reshape(tok_dev, TOPK, D).astype(jnp.float32)
    block_out = (hidden + jnp.sum(gates[:, :, None] * picked_rows, axis=1)).astype(jnp.bfloat16)
    grad_top = grad_out.astype(jnp.float32)
    grad_expert = (gates[:, :, None] * grad_top[:, None, :]).astype(jnp.bfloat16)
    grad_gates = jnp.sum(picked_rows * grad_top[:, None, :], axis=2)
    grad_send = jnp.zeros((EXPERTS * CAP, D), jnp.bfloat16).at[slot].set(grad_expert.reshape(-1, D))
    grad_arrived = lax.all_to_all(
        grad_send.reshape(dp_size, exp_dev * CAP, D), "dp", split_axis=0, concat_axis=0, tiled=True
    ).reshape(dp_size, exp_dev, CAP, D)
    grad_act = jnp.einsum(
        "secd,efd->secf", grad_arrived, down_full, preferred_element_type=jnp.float32
    )
    grad_down = jnp.einsum(
        "secf,secd->efd", act_low, grad_arrived, preferred_element_type=jnp.float32
    )
    sigma = jax.nn.sigmoid(gate_part)
    grad_gate = grad_act * up_part * sigma * (1.0 + gate_part * (1.0 - sigma))
    grad_up = grad_act * gate_part * sigma
    grad_both = jnp.concatenate([grad_gate, grad_up], axis=-1).astype(jnp.bfloat16)
    grad_gate_up = jnp.einsum(
        "secd,secf->edf", arrived, grad_both, preferred_element_type=jnp.float32
    )
    grad_copy = jnp.einsum(
        "secf,edf->secd", grad_both, gate_up, preferred_element_type=jnp.float32
    ).astype(jnp.bfloat16)
    grad_back = lax.all_to_all(
        grad_copy.reshape(dp_size, exp_dev * CAP, D), "dp", split_axis=0, concat_axis=0, tiled=True
    ).reshape(EXPERTS * CAP, D)
    grad_moe = jnp.sum(grad_back[slot].reshape(tok_dev, TOPK, D).astype(jnp.float32), axis=1)
    grad_pick = gates * (grad_gates - jnp.sum(gates * grad_gates, axis=1, keepdims=True))
    grad_logits = jnp.sum(jnp.where(chosen, grad_pick[:, :, None], 0.0), axis=1)
    router_wide = w_router.astype(jnp.float32)
    grad_moe = grad_moe + jnp.einsum("te,de->td", grad_logits, router_wide, precision=HIGH)
    grad_router = jnp.einsum("td,te->de", moe_low.astype(jnp.float32), grad_logits, precision=HIGH)
    unused, moe_pull = jax.vjp(rms_scale, hidden, moe_gain)
    grad_hidden, grad_moe_gain = moe_pull(grad_moe)
    grad_hidden = grad_hidden + grad_top
    grad_hidden_low = grad_hidden.astype(jnp.bfloat16)
    grad_full = lax.all_gather(grad_hidden_low, "mp", axis=0, tiled=True)
    grad_heads = jnp.dot(grad_full, out_part, preferred_element_type=jnp.float32).astype(
        jnp.bfloat16
    )
    grad_out_w = jnp.einsum("rd,rh->dh", grad_full, heads_low, preferred_element_type=jnp.float32)
    grad_query, grad_key, grad_value = lax.map(
        attend_backward,
        (
            grad_heads.reshape(seqs_here, length, head_local * HD),
            query_rot,
            key_rot,
            value_low,
            log_total,
            segments,
        ),
    )
    grad_query = grad_query.reshape(row_count, head_local * HD)
    grad_key = grad_key.reshape(row_count, kv_local * HD)
    grad_value = grad_value.reshape(row_count, kv_local * HD)
    total = jnp.einsum("rh,dh->rd", grad_query, query_full, preferred_element_type=jnp.float32)
    total = total + jnp.einsum("rh,dh->rd", grad_key, key_full, preferred_element_type=jnp.float32)
    grad_normed = lax.psum_scatter(
        (
            total
            + jnp.einsum("rh,dh->rd", grad_value, value_full, preferred_element_type=jnp.float32)
        ).astype(jnp.bfloat16),
        "mp",
        scatter_dimension=0,
        tiled=True,
    ).astype(jnp.float32)
    unused_two, attn_pull = jax.vjp(rms_scale, own_rows, attn_gain)
    grad_own, grad_attn_gain = attn_pull(grad_normed)
    grad_in = grad_own + grad_hidden
    grad_query_w = jnp.einsum(
        "rd,rh->dh", normed_low, grad_query, preferred_element_type=jnp.float32
    )
    grad_key_w = jnp.einsum("rd,rh->dh", normed_low, grad_key, preferred_element_type=jnp.float32)
    grad_value_w = jnp.einsum(
        "rd,rh->dh", normed_low, grad_value, preferred_element_type=jnp.float32
    )
    grad_query_w, grad_key_w, grad_value_w, grad_out_w = (
        lax.psum_scatter(
            grad_query_w.astype(jnp.bfloat16), "dp", scatter_dimension=0, tiled=True
        ).astype(jnp.float32),
        lax.psum_scatter(
            grad_key_w.astype(jnp.bfloat16), "dp", scatter_dimension=0, tiled=True
        ).astype(jnp.float32),
        lax.psum_scatter(
            grad_value_w.astype(jnp.bfloat16), "dp", scatter_dimension=0, tiled=True
        ).astype(jnp.float32),
        lax.psum_scatter(
            grad_out_w.astype(jnp.bfloat16), "dp", scatter_dimension=0, tiled=True
        ).astype(jnp.float32),
    )
    grad_gate_up, grad_down = (
        lax.psum_scatter(
            grad_gate_up.astype(jnp.bfloat16), "mp", scatter_dimension=2, tiled=True
        ).astype(jnp.float32),
        lax.psum_scatter(
            grad_down.astype(jnp.bfloat16), "mp", scatter_dimension=2, tiled=True
        ).astype(jnp.float32),
    )
    grad_attn_gain, grad_moe_gain, grad_router = lax.psum(
        (grad_attn_gain, grad_moe_gain, grad_router), ("dp", "mp")
    )
    return (
        block_out,
        grad_in,
        grad_attn_gain,
        grad_query_w,
        grad_key_w,
        grad_value_w,
        grad_out_w,
        grad_moe_gain,
        grad_router,
        grad_gate_up,
        grad_down,
    )


def solution(mesh):
    placed = (
        P("dp", "mp"),
        P("dp", None),
        P(("dp", "mp"), None),
        P(),
        P("dp", "mp"),
        P("dp", "mp"),
        P("dp", "mp"),
        P("dp", "mp"),
        P(),
        P(),
        P("dp", None, "mp"),
        P("dp", None, "mp"),
        P(("dp", "mp"), None),
    )
    return jax.shard_map(
        local,
        mesh=mesh,
        in_specs=placed,
        out_specs=(
            P(("dp", "mp"), None),
            P(("dp", "mp"), None),
            P(),
            P("dp", "mp"),
            P("dp", "mp"),
            P("dp", "mp"),
            P("dp", "mp"),
            P(),
            P(),
            P("dp", None, "mp"),
            P("dp", None, "mp"),
        ),
        check_vma=False,
    )
```

profile of v0, /device:TPU:0, one launch (start us, length us, event | category | flops | bytes accessed | tf_op | source)
XLA Modules:
  0.0 1211.0 jit_solution(2288261174782326073)
XLA Ops:
  9.3 11.0 all_gather.26
  20.3 9.1 all_gather.25
  29.5 9.2 all_gather.27
  38.7 10.0 all_gather.28
  52.8 5.7 all-gather.5.cloned.1.call-done
  65.9 7.3 fusion.85
  73.3 8.0 fusion.3
  81.3 7.4 fusion.51
  93.0 9.1 reduce-window.19
  105.4 61.4 %reduce-scatter.9.cloned.1.call-done = f32[256,1024]{1,0:T(8,128)} async-done(((f32[1024,1024]{1,0:T(8,128)}), f32[256,1024]{1,0:T(8,128)}) %reduce-scatter.9.cloned.1.call-update) | async-done | bytes 1048592 | tf_op jit(solution)/shard_map/reduce_scatter | solution.py:172
  169.3 13.5 %scatter_custom_fusion = bf16[3072,1024]{1,0:T(8,128)(2,1)} fusion(s32[2048]{0:T(1024)S(1)} %bitcast.226, bf16[]{:T(256)} %constant.132.clone.1, bf16[256,1024]{1,0:T(8,128)(2,1)S(1)} %multiply_convert_fusion.2), kind=kCustom, calls=%fused_computation.54 | custom fusion | bytes 6815746 | tf_op jit(solution)/shard_map/scatter | solution.py:193
  182.9 4.9 all-to-all-start
  189.1 14.7 %scatter_custom_fusion.1 = bf16[3072,1024]{1,0:T(8,128)(2,1)} fusion(s32[2048]{0:T(1024)S(1)} %bitcast.227, f32[256,1024]{1,0:T(8,128)S(1)} %convert_element_type.206, f32[2048]{0:T(1024)S(1)} %div.82, bf16[]{:T(256)} %constant.132.clone.1), kind=kCustom, calls=%fused_computation.50 | custom fusion | flops 4194304 | bytes 7348226 | tf_op jit(solution)/shard_map/scatter | solution.py:217
  203.8 55.6 %all-to-all-done = bf16[8,384,1024]{2,1,0:T(8,128)(2,1)} async-done(((bf16[8,384,1024]{2,1,0:T(8,128)(2,1)}), bf16[8,384,1024]{2,1,0:T(8,128)(2,1)}, u32[]{:S(2)}, u32[]{:S(2)}) %all-to-all-start) | async-done | bytes 6291488 | tf_op jit(solution)/shard_map/all_to_all | solution.py:195
  259.3 4.7 all-to-all-start.2
  264.1 54.0 %all-gather.7.cloned.1.call-done = bf16[4,1024,1024]{2,1,0:T(8,128)(2,1)} async-done(((bf16[4,1024,256]{2,1,0:T(8,128)(2,1)}), bf16[4,1024,1024]{2,1,0:T(8,128)(2,1)}) %all-gather.7.cloned.1.call-update) | async-done | bytes 8388624 | tf_op jit(solution)/shard_map/all_gather | solution.py:199
  318.1 13.8 %fusion.27 = f32[8,4,96,1024]{3,2,0,1:T(8,128)} fusion(bf16[4,1024,1024]{2,1,0:T(8,128)(2,1)} %all-gather.7.cloned.1.call-done, bf16[8,4,96,1024]{3,2,1,0:T(8,128)(2,1)} %bitcast.23), kind=kOutput, calls=%fused_computation.49 | convolution fusion | flops 6442450944 | bytes 27262976 | tf_op jit(solution)/shard_map/secd,edf->secf/dot_general | solution.py:202
  331.9 66.5 %all-gather.9.cloned.1.call-done = bf16[4,512,1024]{2,1,0:T(8,128)(2,1)} async-done(((bf16[4,512,256]{2,1,0:T(8,128)(2,1)}), bf16[4,512,1024]{2,1,0:T(8,128)(2,1)}) %all-gather.9.cloned.1.call-update) | async-done | bytes 4194320 | tf_op jit(solution)/shard_map/all_gather | solution.py:200
  398.3 12.5 %fusion.18 = (bf16[8,4,96,512]{3,2,0,1:T(8,128)(2,1)S(1)}, bf16[8,4,96,512]{3,2,0,1:T(8,128)(2,1)}, bf16[8,4,96,512]{3,2,0,1:T(8,128)(2,1)}) fusion(f32[8,4,96,1024]{3,2,0,1:T(8,128)} %fusion.27, bf16[4,512,1024]{2,1,0:T(8,128)(2,1)} %all-gather.9.cloned.1.call-done, bf16[8,4,96,1024]{3,2,1,0:T(8,128)(2,1)} %bitcast.38), kind=kOutput, calls=%fused_computation.36 | convolution fusion | flops 3246391296 | bytes 32505856 | tf_op jit(solution)/shard_map/secd,efd->secf/dot_general | solution.py:221
  410.9 13.6 %convert_bitcast_fusion = bf16[8,4,96,1024]{3,2,0,1:T(8,128)(2,1)} fusion(bf16[4,1024,1024]{2,1,0:T(8,128)(2,1)} %all-gather.7.cloned.1.call-done, bf16[8,4,96,512]{3,2,0,1:T(8,128)(2,1)} %get-tuple-element.82, bf16[8,4,96,512]{3,2,0,1:T(8,128)(2,1)S(1)} %get-tuple-element.81), kind=kOutput, calls=%fused_computation.41 | convolution fusion | flops 6458179584 | bytes 20971520 | tf_op jit(solution)/shard_map/secf,edf->secd/dot_general | solution.py:234
  424.5 6.6 copy.75
  431.0 4.9 all-to-all-start.3
  436.0 6.6 convert_bitcast_fusion.1
  445.9 61.7 %all-to-all-done.3 = bf16[8,384,1024]{2,1,0:T(8,128)(2,1)} async-done(((bf16[8,384,1024]{2,1,0:T(8,128)(2,1)}), bf16[8,384,1024]{2,1,0:T(8,128)(2,1)}, u32[]{:S(2)}, u32[]{:S(2)}) %all-to-all-start.3) | async-done | bytes 6291488 | tf_op jit(solution)/shard_map/all_to_all | solution.py:237
  507.6 4.7 all-to-all-start.1
  512.4 14.5 %gather_fusion.1 = bf16[2048,1024]{1,0:T(8,128)(2,1)} fusion(bf16[3072,1024]{1,0:T(8,128)(2,1)} %bitcast.44, s32[2048]{0:T(1024)S(1)} %broadcast_clamp_fusion), kind=kCustom, calls=%fused_computation.1 | custom fusion | bytes 8396800 | tf_op jit(solution)/shard_map/gather | solution.py:240
  526.9 6.4 convert_reduce_fusion
  533.3 50.6 %all-to-all-done.1 = bf16[8,384,1024]{2,1,0:T(8,128)(2,1)} async-done(((bf16[8,384,1024]{2,1,0:T(8,128)(2,1)}), bf16[8,384,1024]{2,1,0:T(8,128)(2,1)}, u32[]{:S(2)}, u32[]{:S(2)}) %all-to-all-start.1) | async-done | bytes 6291488 | tf_op jit(solution)/shard_map/all_to_all | solution.py:209
  583.9 14.5 %gather_fusion = bf16[2048,1024]{1,0:T(8,128)(2,1)} fusion(bf16[3072,1024]{1,0:T(8,128)(2,1)} %bitcast.31, s32[2048]{0:T(1024)S(1)} %broadcast_clamp_fusion), kind=kCustom, calls=%fused_computation | custom fusion | bytes 8396800 | tf_op jit(solution)/shard_map/gather | solution.py:212
  598.5 6.1 fusion.6
  609.5 9.5 bitcast_convert_fusion.1
  619.1 32.4 %all-gather.11.cloned.1.call-done = bf16[1024,1024]{1,0:T(8,128)(2,1)} async-done(((bf16[256,1024]{1,0:T(8,128)(2,1)}), bf16[1024,1024]{1,0:T(8,128)(2,1)}) %all-gather.11.cloned.1.call-update) | async-done | bytes 2097168 | tf_op jit(solution)/shard_map/all_gather | solution.py:250
  653.9 15.0 %fusion = (f32[2,2,1024]{2,1,0:T(2,128)S(1)}, f32[2,1024,1024,2]{2,1,3,0:T(8,128)}) fusion(f32[2,2,1024,1024]{2,3,1,0:T(8,128)} %get-tuple-element.100, f32[2,2,1024]{2,1,0:T(2,128)S(1)} %log_add_fusion, bf16[1024,2,64,1]{0,2,3,1:T(8,128)(2,1)S(1)} %bitcast.218, bf16[1024,2,2,64]{0,3,2,1:T(8,128)(2,1)S(1)} %bitcast.213), kind=kOutput, calls=%fused_computation.7 | convolution fusion | flops 549449728 | bytes 34373632 | tf_op jit(solution)/shard_map/while/body/eval_jaxpr/qkgd,skd->kgqs/dot_general | solution.py:103
  671.3 11.0 fusion.2
  682.3 6.9 broadcast_multiply_fusion
  690.1 5.0 convolution_multiply_fusion
  697.1 4.1 fusion.57
  717.9 4.1 fusion.90
  726.5 12.8 %bitcast_convert_fusion = bf16[4,1024,1024]{2,1,0:T(8,128)(2,1)} fusion(bf16[8,4,96,1024]{3,2,1,0:T(8,128)(2,1)} %bitcast.23, bf16[8,4,96,512]{3,2,0,1:T(8,128)(2,1)} %get-tuple-element.82, bf16[8,4,96,512]{3,2,0,1:T(8,128)(2,1)} %copy-done.45), kind=kOutput, calls=%fused_computation.4 | convolution fusion | flops 6459228160 | bytes 20971520 | tf_op jit(solution)/shard_map/secd,secf->edf/dot_general | solution.py:231
  744.1 22.4 %reduce-scatter.17.cloned.1.call-done = bf16[128,128]{1,0:T(8,128)(2,1)} async-done(((bf16[1024,128]{1,0:T(8,128)(2,1)}), bf16[128,128]{1,0:T(8,128)(2,1)}) %reduce-scatter.17.cloned.1.call-update) | async-done | bytes 32784 | tf_op jit(solution)/shard_map/reduce_scatter | solution.py:297
  767.9 35.5 %reduce-scatter.15.cloned.1.call-done = bf16[128,128]{1,0:T(8,128)(2,1)} async-done(((bf16[1024,128]{1,0:T(8,128)(2,1)}), bf16[128,128]{1,0:T(8,128)(2,1)}) %reduce-scatter.15.cloned.1.call-update) | async-done | bytes 32784 | tf_op jit(solution)/shard_map/reduce_scatter | solution.py:294
  804.8 35.8 %reduce-scatter.19.cloned.1.call-done = bf16[128,256]{1,0:T(8,128)(2,1)} async-done(((bf16[1024,256]{1,0:T(8,128)(2,1)}), bf16[128,256]{1,0:T(8,128)(2,1)}) %reduce-scatter.19.cloned.1.call-update) | async-done | bytes 65552 | tf_op jit(solution)/shard_map/reduce_scatter | solution.py:300
  842.1 36.5 %reduce-scatter.13.cloned.1.call-done = bf16[128,256]{1,0:T(8,128)(2,1)} async-done(((bf16[1024,256]{1,0:T(8,128)(2,1)}), bf16[128,256]{1,0:T(8,128)(2,1)}) %reduce-scatter.13.cloned.1.call-update) | async-done | bytes 65552 | tf_op jit(solution)/shard_map/reduce_scatter | solution.py:291
  880.1 45.3 %reduce-scatter.11.cloned.1.call-done = bf16[256,1024]{1,0:T(8,128)(2,1)} async-done(((bf16[1024,1024]{1,0:T(8,128)(2,1)}), bf16[256,1024]{1,0:T(8,128)(2,1)}) %reduce-scatter.11.cloned.1.call-update) | async-done | bytes 524304 | tf_op jit(solution)/shard_map/reduce_scatter | solution.py:271
  930.5 43.2 %all-reduce = (f32[1024]{0:T(1024)}, f32[1024]{0:T(1024)}) all-reduce(f32[1024]{0:T(1024)S(1)} %get-tuple-element.61, f32[1024]{0:T(1024)S(1)} %get-tuple-element.65), channel_id=1, replica_groups=mesh['dp'=8,'mp'=4] {'dp','mp'}, use_global_device_ids=true, to_apply=%region_26.27 | all-reduce | flops 2048 | bytes 16384 | tf_op jit(solution)/shard_map/psum | solution.py:312
  973.7 98.8 %reduce-scatter.21.cloned.1.call-done = bf16[4,1024,256]{2,1,0:T(8,128)(2,1)} async-done(((bf16[4,1024,1024]{2,1,0:T(8,128)(2,1)}), bf16[4,1024,256]{2,1,0:T(8,128)(2,1)}) %reduce-scatter.21.cloned.1.call-update) | async-done | bytes 2097168 | tf_op jit(solution)/shard_map/reduce_scatter | solution.py:305
  1072.5 4.0 convert_element_type.233
  1076.4 126.3 %all-reduce.3.cloned.1.call-done = f32[1024,32]{0,1:T(8,128)} async-done(((f32[1024,32]{0,1:T(8,128)}), f32[1024,32]{0,1:T(8,128)}) %all-reduce.3.cloned.1.call-update) | async-done | bytes 131088 | tf_op jit(solution)/shard_map/psum | solution.py:312
  (210 shorter events, 79.1 us)
Async XLA Ops:
  7.2 181.3 %copy-start = (bf16[1024,32]{0,1:T(8,128)(2,1)S(1)}, bf16[1024,32]{0,1:T(8,128)(2,1)}, u32[]{:S(2)}) copy-start(bf16[1024,32]{0,1:T(8,128)(2,1)} %param.22) | copy-start | bytes 196612
  7.2 53.5 %copy-start.40 = (f32[1024]{0:T(1024)S(1)}, f32[1024]{0:T(1024)}, u32[]{:S(2)}) copy-start(f32[1024]{0:T(1024)} %param.16) | copy-start | bytes 12292
  7.2 51.4 %all-gather.5.cloned.1.call-start = ((), (), s32[]{:S(2)}) async-start(), calls=%async_computation.12 | async-start | bytes 2621440 | tf_op jit(solution)/shard_map/all_gather | solution.py:145
  7.9 158.8 %reduce-scatter.9.cloned.1.call-start = ((), (), s32[]{:S(2)}) async-start(), calls=%async_computation.13 | async-start | bytes 5242880 | tf_op jit(solution)/shard_map/reduce_scatter | solution.py:172
  20.3 43.4 %copy-start.24 = (bf16[1024,128]{1,0:T(8,128)(2,1)}, bf16[1024,128]{1,0:T(8,128)(2,1)S(1)}, u32[]{:S(2)}) copy-start(bf16[1024,128]{1,0:T(8,128)(2,1)S(1)} %all_gather.26) | copy-start | bytes 786436
  29.3 35.2 %copy-start.19 = (bf16[1024,128]{1,0:T(8,128)(2,1)}, bf16[1024,128]{1,0:T(8,128)(2,1)S(1)}, u32[]{:S(2)}) copy-start(bf16[1024,128]{1,0:T(8,128)(2,1)S(1)} %all_gather.25) | copy-start | bytes 786436
  38.7 25.9 %copy-start.10 = (bf16[1024,256]{1,0:T(8,128)(2,1)}, bf16[1024,256]{1,0:T(8,128)(2,1)S(1)}, u32[]{:S(2)}) copy-start(bf16[1024,256]{1,0:T(8,128)(2,1)S(1)} %all_gather.27) | copy-start | bytes 1572868
  48.6 40.1 %copy-start.26 = (bf16[1024,256]{1,0:T(8,128)(2,1)}, bf16[1024,256]{1,0:T(8,128)(2,1)S(1)}, u32[]{:S(2)}) copy-start(bf16[1024,256]{1,0:T(8,128)(2,1)S(1)} %all_gather.28) | copy-start | bytes 1572868
  50.5 15.1 %copy-start.13 = (f32[1024,64]{0,1:T(8,128)}, f32[1024,64]{0,1:T(8,128)S(1)}, u32[]{:S(2)}) copy-start(f32[1024,64]{0,1:T(8,128)S(1)} %get-tuple-element.97) | copy-start | bytes 786436
  50.5 15.1 %copy-start.15 = (f32[1024,64]{0,1:T(8,128)}, f32[1024,64]{0,1:T(8,128)S(1)}, u32[]{:S(2)}) copy-start(f32[1024,64]{0,1:T(8,128)S(1)} %get-tuple-element.98) | copy-start | bytes 786436
  65.6 7.7 copy-start.31
  81.3 7.4 copy-start.38
  88.7 13.3 %copy-start.35 = (bf16[2,64,2,1024]{3,1,2,0:T(8,128)(2,1)}, bf16[2,64,2,1024]{3,1,2,0:T(8,128)(2,1)S(1)}, u32[]{:S(2)}) copy-start(bf16[2,64,2,1024]{3,1,2,0:T(8,128)(2,1)S(1)} %fusion.51) | copy-start | bytes 1572868
  88.8 14.2 %copy-start.3 = (bf16[1024,1024]{1,0:T(8,128)(2,1)S(1)}, bf16[1024,1024]{1,0:T(8,128)(2,1)}, u32[]{:S(2)}) copy-start(bf16[1024,1024]{1,0:T(8,128)(2,1)} %all-gather.5.cloned.1.call-done) | copy-start | bytes 6291460
  91.6 226.5 %all-gather.7.cloned.1.call-start = ((), (), s32[]{:S(2)}) async-start(), calls=%async_computation.14 | async-start | bytes 10485760 | tf_op jit(solution)/shard_map/all_gather | solution.py:199
  92.5 76.7 %copy-start.37 = (f32[1024]{0:T(1024)S(1)}, f32[1024]{0:T(1024)}, u32[]{:S(2)}) copy-start(f32[1024]{0:T(1024)} %param.21) | copy-start | bytes 12292
  169.1 13.7 %copy-start.43 = (f32[256]{0:T(256)}, f32[256]{0:T(256)S(1)}, u32[]{:S(2)}) copy-start(f32[256]{0:T(256)S(1)} %get-tuple-element.69) | copy-start | bytes 3076
  169.3 19.1 %copy-start.8 = (bf16[256,1024]{1,0:T(8,128)(2,1)}, bf16[256,1024]{1,0:T(8,128)(2,1)S(1)}, u32[]{:S(2)}) copy-start(bf16[256,1024]{1,0:T(8,128)(2,1)S(1)} %multiply_convert_fusion.2) | copy-start | bytes 1572868
  182.9 76.5 %all-to-all-start = ((bf16[8,384,1024]{2,1,0:T(8,128)(2,1)}), bf16[8,384,1024]{2,1,0:T(8,128)(2,1)}, u32[]{:S(2)}, u32[]{:S(2)}) async-start(bf16[8,384,1024]{2,1,0:T(8,128)(2,1)} %bitcast.201), calls=%async_computation.1 | async-start | bytes 12582912 | tf_op jit(solution)/shard_map/all_to_all | solution.py:195
  187.8 210.6 %all-gather.9.cloned.1.call-start = ((), (), s32[]{:S(2)}) async-start(), calls=%async_computation.15 | async-start | bytes 5242880 | tf_op jit(solution)/shard_map/all_gather | solution.py:200
  259.3 139.0 %all-to-all-start.2 = ((bf16[8,384,1024]{2,1,0:T(8,128)(2,1)}), bf16[8,384,1024]{2,1,0:T(8,128)(2,1)}, u32[]{:S(2)}, u32[]{:S(2)}) async-start(bf16[8,384,1024]{2,1,0:T(8,128)(2,1)} %bitcast.202), calls=%async_computation.3 | async-start | bytes 12582912 | tf_op jit(solution)/shard_map/all_to_all | solution.py:218
  410.9 13.6 %copy-start.45 = (bf16[8,4,96,512]{3,2,0,1:T(8,128)(2,1)}, bf16[8,4,96,512]{3,2,0,1:T(8,128)(2,1)S(1)}, u32[]{:S(2)}) copy-start(bf16[8,4,96,512]{3,2,0,1:T(8,128)(2,1)S(1)} %get-tuple-element.81) | copy-start | bytes 9437188
  431.0 76.5 %all-to-all-start.3 = ((bf16[8,384,1024]{2,1,0:T(8,128)(2,1)}), bf16[8,384,1024]{2,1,0:T(8,128)(2,1)}, u32[]{:S(2)}, u32[]{:S(2)}) async-start(bf16[8,384,1024]{2,1,0:T(8,128)(2,1)} %bitcast.204), calls=%async_computation.4 | async-start | bytes 12582912 | tf_op jit(solution)/shard_map/all_to_all | solution.py:237
  507.6 76.4 %all-to-all-start.1 = ((bf16[8,384,1024]{2,1,0:T(8,128)(2,1)}), bf16[8,384,1024]{2,1,0:T(8,128)(2,1)}, u32[]{:S(2)}, u32[]{:S(2)}) async-start(bf16[8,384,1024]{2,1,0:T(8,128)(2,1)} %bitcast.203), calls=%async_computation.2 | async-start | bytes 12582912 | tf_op jit(solution)/shard_map/all_to_all | solution.py:209
  512.3 139.2 %all-gather.11.cloned.1.call-start = ((), (), s32[]{:S(2)}) async-start(), calls=%async_computation.16 | async-start | bytes 2621440 | tf_op jit(solution)/shard_map/all_gather | solution.py:250
  598.5 8.4 copy-start.44
  609.0 10.1 copy-start.39
  609.0 42.5 %copy-start.27 = (bf16[1024,256]{1,0:T(8,128)(2,1)S(1)}, bf16[1024,256]{1,0:T(8,128)(2,1)}, u32[]{:S(2)}) copy-start(bf16[1024,256]{1,0:T(8,128)(2,1)} %copy-done.26) | copy-start | bytes 1572868
  609.0 132.3 %reduce-scatter.23.cloned.1.call-start = ((), (), s32[]{:S(2)}) async-start(), calls=%async_computation.24 | async-start | bytes 5242880 | tf_op jit(solution)/shard_map/reduce_scatter | solution.py:308
  619.0 147.5 %reduce-scatter.17.cloned.1.call-start = ((), (), s32[]{:S(2)}) async-start(), calls=%async_computation.20 | async-start | bytes 294912 | tf_op jit(solution)/shard_map/reduce_scatter | solution.py:297
  653.9 15.1 %copy-start.25 = (bf16[1024,256]{0,1:T(8,128)(2,1)}, bf16[1024,256]{0,1:T(8,128)(2,1)S(1)}, u32[]{:S(2)}) copy-start(bf16[1024,256]{0,1:T(8,128)(2,1)S(1)} %convolution_convert_fusion.2) | copy-start | bytes 1572868
  653.9 15.1 %slice-start = ((s8[16777216]{0:T(1024)(128)(4,1)}), s8[4194304]{0:T(1024)(128)(4,1)S(1)}, s32[]{:S(2)}) async-start(s8[16777216]{0:T(1024)(128)(4,1)} %bitcast.199), calls=%async_computation.25 | async-start | bytes 8388608
  653.9 15.1 %slice-start.1 = ((s8[16777216]{0:T(1024)(128)(4,1)}), s8[4194304]{0:T(1024)(128)(4,1)S(1)}, s32[]{:S(2)}) async-start(s8[16777216]{0:T(1024)(128)(4,1)} %bitcast.199), calls=%async_computation.26 | async-start | bytes 8388608
  653.9 16.2 %slice-start.2 = ((s8[16777216]{0:T(1024)(128)(4,1)}), s8[4194304]{0:T(1024)(128)(4,1)S(1)}, s32[]{:S(2)}) async-start(s8[16777216]{0:T(1024)(128)(4,1)} %bitcast.199), calls=%async_computation.27 | async-start | bytes 8388608
  653.9 17.4 %slice-start.3 = ((s8[16777216]{0:T(1024)(128)(4,1)}), s8[4194304]{0:T(1024)(128)(4,1)S(1)}, s32[]{:S(2)}) async-start(s8[16777216]{0:T(1024)(128)(4,1)} %bitcast.199), calls=%async_computation.28 | async-start | bytes 8388608
  671.3 11.0 copy-start.21
  671.3 11.0 copy-start.29
  682.3 7.8 copy-start.32
  703.4 100.0 %reduce-scatter.15.cloned.1.call-start = ((), (), s32[]{:S(2)}) async-start(), calls=%async_computation.19 | async-start | bytes 294912 | tf_op jit(solution)/shard_map/reduce_scatter | solution.py:294
  705.6 8.5 copy-start.16
  707.1 133.5 %reduce-scatter.19.cloned.1.call-start = ((), (), s32[]{:S(2)}) async-start(), calls=%async_computation.21 | async-start | bytes 589824 | tf_op jit(solution)/shard_map/reduce_scatter | solution.py:300
  712.7 165.8 %reduce-scatter.13.cloned.1.call-start = ((), (), s32[]{:S(2)}) async-start(), calls=%async_computation.18 | async-start | bytes 589824 | tf_op jit(solution)/shard_map/reduce_scatter | solution.py:291
  721.9 203.4 %reduce-scatter.11.cloned.1.call-start = ((), (), s32[]{:S(2)}) async-start(), calls=%async_computation.17 | async-start | bytes 2621440 | tf_op jit(solution)/shard_map/reduce_scatter | solution.py:271
  726.4 346.1 %reduce-scatter.21.cloned.1.call-start = ((), (), s32[]{:S(2)}) async-start(), calls=%async_computation.23 | async-start | bytes 10485760 | tf_op jit(solution)/shard_map/reduce_scatter | solution.py:305
  739.2 186.1 %copy-start.41 = (f32[1024]{0:T(1024)S(1)}, f32[1024]{0:T(1024)}, u32[]{:S(2)}) copy-start(f32[1024]{0:T(1024)} %param.16) | copy-start | bytes 12292
  739.2 187.8 %copy-start.6 = (f32[256,1024]{1,0:T(8,128)S(1)}, f32[256,1024]{1,0:T(8,128)}, u32[]{:S(2)}) copy-start(f32[256,1024]{1,0:T(8,128)} %copy-done.5) | copy-start | bytes 3145732
  739.3 187.8 %copy-start.12 = (bf16[256,1024]{1,0:T(8,128)(2,1)S(1)}, bf16[256,1024]{1,0:T(8,128)(2,1)}, u32[]{:S(2)}) copy-start(bf16[256,1024]{1,0:T(8,128)(2,1)} %param.25) | copy-start | bytes 1572868
  739.3 463.4 %all-reduce.3.cloned.1.call-start = ((), (), s32[]{:S(2)}) async-start(), calls=%async_computation.22 | async-start | bytes 262144 | tf_op jit(solution)/shard_map/psum | solution.py:312
  (19 other events, 64.6 us)
Sparse Core Ops, SparseCore 0:
  9.6 48.9 all-gather.4
  91.7 75.0 reduce-scatter.8
  168.4 149.5 all-gather.6
  319.6 78.7 all-gather.8
  609.1 42.3 all-gather.10
  653.8 75.4 reduce-scatter.22
  732.3 34.1 reduce-scatter.16
  769.8 33.5 reduce-scatter.14
  806.5 34.1 reduce-scatter.18
  844.4 34.1 reduce-scatter.12
  881.5 43.8 reduce-scatter.10
  927.7 144.7 reduce-scatter.20
  1079.5 123.1 all-reduce.2
where the time goes:
time: 1220 us; the launch traced here: 1210 us
  waiting for transfers between devices  790 us (65%)
  matrix products  141 us (12%)
  other arithmetic  98.1 us (8%)
  blocking collectives  82.4 us (7%)
  local copies, waits for them, and re-layouts  63.5 us (5%)
  starting transfers between devices  20.6 us (2%)
  between operations  14.9 us (1%)
    psum x1, waiting for transfers between devices, local(): lax.psum((grad_attn_gain, grad_moe_gain, grad_router), ('dp', 'mp'))  126 us
    reduce_scatter x1, waiting for transfers between devices, local(): lax.psum_scatter(grad_gate_up.astype(jnp.bfloat16), 'mp', scatter_dimensi...  98.8 us
    all_gather x1, waiting for transfers between devices, local(): lax.all_gather(w_down, 'mp', axis=2, tiled=True)  66.5 us
    all_to_all x1, waiting for transfers between devices, local(): lax.all_to_all(grad_copy.reshape(dp_size, exp_dev * CAP, D), 'dp', split_...  61.7 us
    reduce_scatter x1, waiting for transfers between devices, local(): lax.psum_scatter(jnp.einsum('rh,dh->rd', heads_low, out_part, preferred_e...  61.4 us
    all_to_all x1, waiting for transfers between devices, local(): lax.all_to_all(send_rows.reshape(dp_size, exp_dev * CAP, D), 'dp', split_...  55.6 us
    all_gather x1, waiting for transfers between devices, local(): lax.all_gather(w_gate_up, 'mp', axis=2, tiled=True)  54 us
    all_to_all x1, waiting for transfers between devices, local(): lax.all_to_all(expert_out.reshape(dp_size, exp_dev * CAP, D), 'dp', split...  50.6 us
  transfers between devices with their start and end apart: 17, of which 15 were waited for; matrix products, arithmetic and copies ran while one was open for 17% of the time, Pallas kernels for 0%

commit v1 on v0

v1 whole, which is shorter than its diff:
```python
import functools
import math

import jax
import jax.numpy as jnp
from jax import lax
from jax.experimental import pallas as pl
from jax.experimental.pallas import tpu as pltpu
from jax.sharding import PartitionSpec as P

D = 1024
HD = 64
EXPERTS = 32
FF = 512
TOPK = 8
CAP = 96


EPS = 1e-06
ROPE_BASE = 10000.0
NEG_FILL = -1000000000.0
HIGH = lax.Precision.HIGHEST


def rms_scale(values, gain):
    return values * lax.rsqrt(jnp.mean(values * values, axis=-1, keepdims=True) + EPS) * gain


def positions_of(seg_row):
    index = jnp.arange(seg_row.shape[0], dtype=jnp.int32)
    change = jnp.concatenate([jnp.ones((1,), dtype=bool), seg_row[1:] != seg_row[:-1]])
    begin = lax.cummax(jnp.where(change, index, jnp.zeros_like(index)), axis=0)
    return index - begin


def angles(seg_row):
    place = positions_of(seg_row).astype(jnp.float32)
    freq = ROPE_BASE ** (-jnp.arange(0, HD, 2).astype(jnp.float32) / HD)
    theta = place[:, None] * freq[None, :]
    theta = jnp.concatenate([theta, theta], axis=1)
    return (jnp.cos(theta)[:, None, :], jnp.sin(theta)[:, None, :])


def rotate(values, cosine, sine):
    half = values.shape[-1] // 2
    turned = jnp.concatenate([-values[..., half:], values[..., :half]], axis=-1)
    return values * cosine + turned * sine


def unrotate(values, cosine, sine):
    half = values.shape[-1] // 2
    spun = values * sine
    return values * cosine + jnp.concatenate([spun[..., half:], -spun[..., :half]], axis=-1)


def allowed_pairs(seg_row):
    index = jnp.arange(seg_row.shape[0], dtype=jnp.int32)
    return (seg_row[:, None] == seg_row[None, :]) & (index[:, None] >= index[None, :])


def attend_forward(packed):
    query, key, value, seg_row = packed
    length = seg_row.shape[0]
    cosine, sine = angles(seg_row)
    query_rot = rotate(query, cosine, sine).astype(jnp.bfloat16)
    key_rot = rotate(key, cosine, sine).astype(jnp.bfloat16)
    value_low = value.astype(jnp.bfloat16)
    grouped = query_rot.reshape(length, key.shape[1], -1, HD)
    scores = jnp.einsum("qkgd,skd->kgqs", grouped, key_rot, preferred_element_type=jnp.float32) * (
        1.0 / math.sqrt(HD)
    )
    scores = jnp.where(allowed_pairs(seg_row), scores, NEG_FILL)
    top_score = jnp.max(scores, axis=-1, keepdims=True)
    expos = jnp.exp(scores - top_score)
    totals = jnp.sum(expos, axis=-1, keepdims=True)
    probs_low = (expos / totals).astype(jnp.bfloat16)
    mixed = jnp.einsum("kgqs,skd->qkgd", probs_low, value_low, preferred_element_type=jnp.float32)
    log_total = top_score + jnp.log(totals)
    return (
        mixed.reshape(length, -1).astype(jnp.bfloat16),
        log_total,
        query_rot,
        key_rot,
        value_low,
    )


def attend_backward(packed):
    grad_mixed, query_rot, key_rot, value_low, log_total, seg_row = packed
    length = seg_row.shape[0]
    kv_heads = key_rot.shape[1]
    scale = 1.0 / math.sqrt(HD)
    grouped = query_rot.reshape(length, kv_heads, -1, HD)
    scores = (
        jnp.einsum("qkgd,skd->kgqs", grouped, key_rot, preferred_element_type=jnp.float32) * scale
    )
    scores = jnp.where(allowed_pairs(seg_row), scores, NEG_FILL)
    probs = jnp.exp(scores - log_total)
    grad_grouped = grad_mixed.reshape(length, kv_heads, -1, HD)
    grad_value = jnp.einsum(
        "kgqs,qkgd->skd",
        probs.astype(jnp.bfloat16),
        grad_grouped,
        preferred_element_type=jnp.float32,
    )
    grad_probs = jnp.einsum(
        "qkgd,skd->kgqs", grad_grouped, value_low, preferred_element_type=jnp.float32
    )
    centre = jnp.sum(probs * grad_probs, axis=-1, keepdims=True)
    grad_scores = (probs * (grad_probs - centre)).astype(jnp.bfloat16)
    grad_query = (
        jnp.einsum("kgqs,skd->qkgd", grad_scores, key_rot, preferred_element_type=jnp.float32)
        * scale
    )
    grad_key = (
        jnp.einsum("kgqs,qkgd->skd", grad_scores, grouped, preferred_element_type=jnp.float32)
        * scale
    )
    cosine, sine = angles(seg_row)
    grad_query = unrotate(grad_query.reshape(length, -1, HD), cosine, sine)
    grad_key = unrotate(grad_key, cosine, sine)
    return (
        grad_query.reshape(length, -1).astype(jnp.bfloat16),
        grad_key.reshape(length, -1).astype(jnp.bfloat16),
        grad_value.reshape(length, -1).astype(jnp.bfloat16),
    )


MESH = pl.DeviceIdType.MESH
VMEM_ASK = 56 * 1024 * 1024


def flip(index, bit):
    return index + bit - 2 * bit * ((index // bit) % 2)


def orders_of(size):
    bits = [1 << k for k in range(size.bit_length() - 1)]
    rest = bits[1:]
    cut = len(rest) // 2
    near, far = rest[:cut], rest[cut:]
    return [bits[:1] + near + far, bits[:1] + far + near]


def flip_any(index, mask):
    bit = 1
    while bit <= mask:
        if mask & bit:
            index = flip(index, bit)
        bit *= 2
    return index


def greet_cube(axis, me, size):
    barrier = pltpu.get_barrier_semaphore()
    bits = [1 << k for k in range(size.bit_length() - 1)]
    for bit in bits:
        pl.semaphore_signal(barrier, inc=1, device_id={axis: flip(me, bit)}, device_id_type=MESH)
    pl.semaphore_wait(barrier, len(bits))


def gather_kernel(axis, size, count, *refs):
    ins, outs, sems = refs[:count], refs[count : 2 * count], refs[2 * count :]
    me = lax.axis_index(axis)
    greet_cube(axis, me, size)
    for a in range(count):
        outs[a][me] = ins[a][...]
    orders = [order[::-1] for order in orders_of(size)]
    held = [[0], [0]]
    for phase in range(len(orders[0])):
        copies = []
        for a in range(count):
            half = ins[a].shape[0] // 2
            for part in range(2):
                bit = orders[part][phase]
                for mask in held[part]:
                    view = outs[a].at[flip_any(me, mask), pl.ds(part * half, half)]
                    copies.append(
                        pltpu.make_async_remote_copy(
                            src_ref=view,
                            dst_ref=view,
                            send_sem=sems[0].at[a, part, mask | bit],
                            recv_sem=sems[1].at[a, part, mask | bit],
                            device_id={axis: flip(me, bit)},
                            device_id_type=MESH,
                        )
                    )
        for copy in copies:
            copy.start()
        for copy in copies:
            copy.wait()
        held = [
            held[part] + [mask | orders[part][phase] for mask in held[part]] for part in range(2)
        ]


def params(number):
    return pltpu.CompilerParams(
        collective_id=number, has_side_effects=True, vmem_limit_bytes=VMEM_ASK
    )


def cost(byte_count):
    return pl.CostEstimate(flops=0, bytes_accessed=byte_count, transcendentals=0)


def cube_gather(arrays, axis, number):
    size = lax.axis_size(axis)
    count = len(arrays)
    return pl.pallas_call(
        functools.partial(gather_kernel, axis, size, count),
        out_shape=[jax.ShapeDtypeStruct((size,) + a.shape, a.dtype) for a in arrays],
        in_specs=[pl.BlockSpec(memory_space=pltpu.VMEM)] * count,
        out_specs=[pl.BlockSpec(memory_space=pltpu.VMEM)] * count,
        scratch_shapes=[pltpu.SemaphoreType.DMA((count, 2, size))] * 2,
        compiler_params=params(number),
        cost_estimate=cost(60000000),
        name="cube_gather",
    )(*arrays)


def scatter_kernel(axis, size, count, *refs):
    ins, outs = refs[:count], refs[count : 2 * count]
    got, keep = refs[2 * count : 3 * count], refs[3 * count : 4 * count]
    sems = refs[4 * count :]
    me = lax.axis_index(axis)
    greet_cube(axis, me, size)
    orders = orders_of(size)
    live = [list(range(size)), list(range(size))]
    phases = len(orders[0])
    for phase in range(phases):
        copies = []
        for a in range(count):
            half = outs[a].shape[0] // 2
            for part in range(2):
                bit = orders[part][phase]
                rows = pl.ds(part * half, half)
                for mask in live[part]:
                    if not mask & bit:
                        continue
                    if phase == 0:
                        source = ins[a].at[flip_any(me, mask), rows]
                    else:
                        source = keep[a].at[mask // 2, rows]
                    copies.append(
                        pltpu.make_async_remote_copy(
                            src_ref=source,
                            dst_ref=got[a].at[mask, rows],
                            send_sem=sems[0].at[a, part, mask],
                            recv_sem=sems[1].at[a, part, mask],
                            device_id={axis: flip(me, bit)},
                            device_id_type=MESH,
                        )
                    )
        for copy in copies:
            copy.start()
        for copy in copies:
            copy.wait()
        for a in range(count):
            half = outs[a].shape[0] // 2
            for part in range(2):
                bit = orders[part][phase]
                rows = pl.ds(part * half, half)
                stay = [mask for mask in live[part] if not mask & bit]
                for mask in stay:
                    if phase == 0:
                        own = ins[a][flip_any(me, mask), rows]
                    else:
                        own = keep[a][mask // 2, rows]
                    total = own.astype(jnp.float32) + got[a][mask | bit, rows].astype(jnp.float32)
                    if phase == phases - 1:
                        outs[a][rows] = total
                    else:
                        keep[a][mask // 2, rows] = total.astype(keep[a].dtype)
        live = [[m for m in live[part] if not m & orders[part][phase]] for part in range(2)]


def cube_scatter(arrays, axis, number):
    size = lax.axis_size(axis)
    count = len(arrays)
    slots = [pltpu.VMEM(a.shape, a.dtype) for a in arrays]
    return pl.pallas_call(
        functools.partial(scatter_kernel, axis, size, count),
        out_shape=[jax.ShapeDtypeStruct(a.shape[1:], jnp.float32) for a in arrays],
        in_specs=[pl.BlockSpec(memory_space=pltpu.VMEM)] * count,
        out_specs=[pl.BlockSpec(memory_space=pltpu.VMEM)] * count,
        scratch_shapes=slots
        + [pltpu.VMEM((size // 2,) + a.shape[1:], a.dtype) for a in arrays]
        + [pltpu.SemaphoreType.DMA((count, 2, size))] * 2,
        compiler_params=params(number),
        cost_estimate=cost(60000000),
        name="cube_scatter",
    )(*arrays)


def greet_line(axis, me, size):
    barrier = pltpu.get_barrier_semaphore()
    for ok, other in ((me < size - 1, me + 1), (me > 0, me - 1)):

        @pl.when(ok)
        def _(other=other):
            pl.semaphore_signal(barrier, inc=1, device_id={axis: other}, device_id_type=MESH)

    inner = (me < size - 1) & (me > 0)

    @pl.when(inner)
    def _():
        pl.semaphore_wait(barrier, 2)

    @pl.when(jnp.logical_not(inner))
    def _():
        pl.semaphore_wait(barrier, 1)


def line_gather_kernel(axis, size, x_ref, out_ref, send_sem, recv_sem):
    me = lax.axis_index(axis)
    greet_line(axis, me, size)
    out_ref[me] = x_ref[...]

    def copy_of(way, step, block, target):
        return pltpu.make_async_remote_copy(
            src_ref=out_ref.at[block],
            dst_ref=out_ref.at[block],
            send_sem=send_sem.at[way, step],
            recv_sem=recv_sem.at[way, step],
            device_id={axis: target},
            device_id_type=MESH,
        )

    for step in range(size - 1):

        @pl.when((me - step >= 0) & (me < size - 1))
        def _(step=step):
            copy_of(0, step, me - step, me + 1).start()

        @pl.when((me + step <= size - 1) & (me > 0))
        def _(step=step):
            copy_of(1, step, me + step, me - 1).start()

        @pl.when(me - 1 - step >= 0)
        def _(step=step):
            copy_of(0, step, me - 1 - step, me - 1).wait_recv()

        @pl.when(me + 1 + step <= size - 1)
        def _(step=step):
            copy_of(1, step, me + 1 + step, me + 1).wait_recv()

    for step in range(size - 1):

        @pl.when((me - step >= 0) & (me < size - 1))
        def _(step=step):
            copy_of(0, step, me - step, me + 1).wait_send()

        @pl.when((me + step <= size - 1) & (me > 0))
        def _(step=step):
            copy_of(1, step, me + step, me - 1).wait_send()


def line_gather(array, axis, number):
    size = lax.axis_size(axis)
    return pl.pallas_call(
        functools.partial(line_gather_kernel, axis, size),
        out_shape=jax.ShapeDtypeStruct((size,) + array.shape, array.dtype),
        in_specs=[pl.BlockSpec(memory_space=pltpu.VMEM)],
        out_specs=pl.BlockSpec(memory_space=pltpu.VMEM),
        scratch_shapes=[pltpu.SemaphoreType.DMA((2, size))] * 2,
        compiler_params=params(number),
        cost_estimate=cost(80000000),
        name="line_gather",
    )(array)


def line_scatter_kernel(axis, size, x_ref, out_ref, stage, got, send_sem, recv_sem):
    me = lax.axis_index(axis)
    greet_line(axis, me, size)

    def copy_of(way, dest, target):
        return pltpu.make_async_remote_copy(
            src_ref=stage.at[way, dest],
            dst_ref=got.at[way, dest],
            send_sem=send_sem.at[way, dest],
            recv_sem=recv_sem.at[way, dest],
            device_id={axis: target},
            device_id_type=MESH,
        )

    def pass_on(way, dest, source, target, first):
        @pl.when(first)
        def _():
            stage[way, dest] = x_ref[dest]

        @pl.when(jnp.logical_not(first))
        def _():
            copy_of(way, dest, source).wait_recv()
            stage[way, dest] = (
                x_ref[dest].astype(jnp.float32) + got[way, dest].astype(jnp.float32)
            ).astype(stage.dtype)

        copy_of(way, dest, target).start()

    for k in range(size - 1):
        up, down = size - 1 - k, k

        @pl.when(me < up)
        def _(up=up):
            pass_on(0, up, me - 1, me + 1, me == 0)

        @pl.when(me > down)
        def _(down=down):
            pass_on(1, down, me + 1, me - 1, me == size - 1)

    out_ref[...] = x_ref[me].astype(jnp.float32)

    @pl.when(me > 0)
    def _():
        copy_of(0, me, me - 1).wait_recv()
        out_ref[...] += got[0, me].astype(jnp.float32)

    @pl.when(me < size - 1)
    def _():
        copy_of(1, me, me + 1).wait_recv()
        out_ref[...] += got[1, me].astype(jnp.float32)

    for k in range(size - 1):
        up, down = size - 1 - k, k

        @pl.when(me < up)
        def _(up=up):
            copy_of(0, up, me + 1).wait_send()

        @pl.when(me > down)
        def _(down=down):
            copy_of(1, down, me - 1).wait_send()


def line_scatter(array, axis, number):
    size = lax.axis_size(axis)
    return pl.pallas_call(
        functools.partial(line_scatter_kernel, axis, size),
        out_shape=jax.ShapeDtypeStruct(array.shape[1:], jnp.float32),
        in_specs=[pl.BlockSpec(memory_space=pltpu.VMEM)],
        out_specs=pl.BlockSpec(memory_space=pltpu.VMEM),
        scratch_shapes=[pltpu.VMEM((2,) + array.shape, array.dtype)] * 2
        + [pltpu.SemaphoreType.DMA((2, size))] * 2,
        compiler_params=params(number),
        cost_estimate=cost(80000000),
        name="line_scatter",
    )(array)


def total_kernel(sizes, x_ref, out_ref, got, sent, send_sem, recv_sem):
    steps = []
    for axis, size in sizes:
        steps += [(axis, 1 << k) for k in range(size.bit_length() - 1)]
    barrier = pltpu.get_barrier_semaphore()
    for axis, bit in steps:
        pl.semaphore_signal(
            barrier,
            inc=1,
            device_id={axis: flip(lax.axis_index(axis), bit)},
            device_id_type=MESH,
        )
    pl.semaphore_wait(barrier, len(steps))
    sent[0] = x_ref[...]
    for k, (axis, bit) in enumerate(steps):
        copy = pltpu.make_async_remote_copy(
            src_ref=sent.at[k],
            dst_ref=got.at[k],
            send_sem=send_sem.at[k],
            recv_sem=recv_sem.at[k],
            device_id={axis: flip(lax.axis_index(axis), bit)},
            device_id_type=MESH,
        )
        copy.start()
        copy.wait()
        if k == len(steps) - 1:
            out_ref[...] = sent[k] + got[k]
        else:
            sent[k + 1] = sent[k] + got[k]


def total_of(array, axes, number):
    sizes = [(axis, lax.axis_size(axis)) for axis in axes]
    count = sum(size.bit_length() - 1 for _, size in sizes)
    return pl.pallas_call(
        functools.partial(total_kernel, sizes),
        out_shape=jax.ShapeDtypeStruct(array.shape, array.dtype),
        in_specs=[pl.BlockSpec(memory_space=pltpu.VMEM)],
        out_specs=pl.BlockSpec(memory_space=pltpu.VMEM),
        scratch_shapes=[pltpu.VMEM((count,) + array.shape, array.dtype)] * 2
        + [pltpu.SemaphoreType.DMA((count,))] * 2,
        compiler_params=params(number),
        cost_estimate=cost(60000000),
        name="total",
    )(array)


def local(
    block_in,
    segments,
    routes,
    attn_gain,
    w_query,
    w_key,
    w_value,
    w_out,
    moe_gain,
    w_router,
    w_gate_up,
    w_down,
    grad_out,
):
    dp_size = lax.axis_size("dp")
    mp_index = lax.axis_index("mp")
    dp_index = lax.axis_index("dp")
    tok_dev = routes.shape[0]
    seqs_here = segments.shape[0]
    exp_dev = EXPERTS // dp_size
    gate_up = lax.all_gather(w_gate_up, "mp", axis=2, tiled=True)
    down_full = lax.all_gather(w_down, "mp", axis=2, tiled=True)
    stacked = line_gather(block_in, "mp", 1)
    full_rows = stacked.transpose(1, 0, 2).reshape(block_in.shape[0], -1)
    row_count = full_rows.shape[0]
    length = row_count // seqs_here
    wide = full_rows.astype(jnp.float32)
    normed_low = rms_scale(wide, attn_gain).astype(jnp.bfloat16)
    q_cols, k_cols = w_query.shape[1], w_key.shape[1]
    packed = jnp.concatenate([w_query, w_key, w_value, w_out], axis=1)
    (gathered,) = cube_gather([packed], "dp", 2)
    gathered = gathered.reshape(-1, packed.shape[1])
    qkv_cols = q_cols + 2 * k_cols
    qkv_full = gathered[:, :qkv_cols]
    out_part = gathered[:, qkv_cols:]
    qkv = jnp.dot(normed_low, qkv_full, preferred_element_type=jnp.float32)
    query = qkv[:, :q_cols]
    key = qkv[:, q_cols : q_cols + k_cols]
    value = qkv[:, q_cols + k_cols :]
    head_local = q_cols // HD
    kv_local = k_cols // HD
    mixed, log_total, query_rot, key_rot, value_low = lax.map(
        attend_forward,
        (
            query.reshape(seqs_here, length, head_local, HD),
            key.reshape(seqs_here, length, kv_local, HD),
            value.reshape(seqs_here, length, kv_local, HD),
            segments,
        ),
    )
    heads_low = mixed.reshape(row_count, head_local * HD)
    row_start = mp_index * tok_dev
    attn_mixed = line_scatter(
        jnp.einsum("rh,dh->rd", heads_low, out_part, preferred_element_type=jnp.float32)
        .astype(jnp.bfloat16)
        .reshape(-1, tok_dev, D),
        "mp",
        3,
    )
    own_rows = lax.dynamic_slice_in_dim(wide, row_start, tok_dev, 0)
    hidden = own_rows + attn_mixed
    moe_low = rms_scale(hidden, moe_gain).astype(jnp.bfloat16)
    logits = jnp.dot(moe_low, w_router, preferred_element_type=jnp.float32)
    used = jnp.sum(
        (routes[:, :, None] == jnp.arange(EXPERTS, dtype=jnp.int32)[None, None, :]).astype(
            jnp.float32
        ),
        axis=1,
    )
    routed = used > 0.0
    top_logit = jnp.max(jnp.where(routed, logits, NEG_FILL), axis=1, keepdims=True)
    raised = jnp.where(routed, jnp.exp(jnp.where(routed, logits - top_logit, 0.0)), 0.0)
    gates = raised / jnp.sum(raised, axis=1, keepdims=True)
    order = jnp.arange(tok_dev, dtype=jnp.int32)
    before = (order[:, None] > order[None, :]).astype(jnp.bfloat16)
    rank = jnp.dot(before, used.astype(jnp.bfloat16), preferred_element_type=jnp.float32)
    rank = jnp.where(routed, rank, -1.0)
    info = jnp.concatenate(
        [gates, rank, jnp.zeros((tok_dev, 128 - 2 * EXPERTS), jnp.float32)], axis=1
    )
    tokens, tops, infos = cube_gather([moe_low, grad_out, info], "dp", 4)
    first = dp_index * exp_dev
    gate_cols = lax.dynamic_slice_in_dim(infos, first, exp_dev, 2)
    rank_cols = lax.dynamic_slice_in_dim(infos, EXPERTS + first, exp_dev, 2)
    gate_cols = gate_cols.transpose(0, 2, 1)
    rank_cols = rank_cols.transpose(0, 2, 1)
    place = jnp.arange(CAP, dtype=jnp.float32)[None, None, :, None]
    picks_wide = rank_cols[:, :, None, :] == place
    picks = picks_wide.astype(jnp.bfloat16)
    slot_gates = jnp.sum(jnp.where(picks_wide, gate_cols[:, :, None, :], 0.0), axis=3)
    arrived = jnp.einsum(
        "sect,std->secd", picks, tokens, preferred_element_type=jnp.float32
    ).astype(jnp.bfloat16)
    top_rows = jnp.einsum("sect,std->secd", picks, tops, preferred_element_type=jnp.float32)
    grad_arrived = (slot_gates[..., None] * top_rows).astype(jnp.bfloat16)
    both = jnp.einsum("secd,edf->secf", arrived, gate_up, preferred_element_type=jnp.float32)
    gate_part = both[..., :FF]
    up_part = both[..., FF:]
    act_low = (jax.nn.silu(gate_part) * up_part).astype(jnp.bfloat16)
    expert_out = jnp.einsum(
        "secf,efd->secd", act_low, down_full, preferred_element_type=jnp.float32
    ).astype(jnp.bfloat16)
    grad_slots = jnp.sum(top_rows * expert_out.astype(jnp.float32), axis=3)
    scaled_out = (slot_gates[..., None] * expert_out.astype(jnp.float32)).astype(jnp.bfloat16)
    part_out = jnp.einsum(
        "sect,secd->std", picks, scaled_out, preferred_element_type=jnp.float32
    ).astype(jnp.bfloat16)
    grad_act = jnp.einsum(
        "secd,efd->secf", grad_arrived, down_full, preferred_element_type=jnp.float32
    )
    grad_down = jnp.einsum(
        "secf,secd->efd", act_low, grad_arrived, preferred_element_type=jnp.float32
    )
    grad_down = lax.psum_scatter(
        grad_down.astype(jnp.bfloat16), "mp", scatter_dimension=2, tiled=True
    ).astype(jnp.float32)
    sigma = jax.nn.sigmoid(gate_part)
    grad_gate = grad_act * up_part * sigma * (1.0 + gate_part * (1.0 - sigma))
    grad_up = grad_act * gate_part * sigma
    grad_both = jnp.concatenate([grad_gate, grad_up], axis=-1).astype(jnp.bfloat16)
    grad_gate_up = jnp.einsum(
        "secd,secf->edf", arrived, grad_both, preferred_element_type=jnp.float32
    )
    grad_gate_up = lax.psum_scatter(
        grad_gate_up.astype(jnp.bfloat16), "mp", scatter_dimension=2, tiled=True
    ).astype(jnp.float32)
    grad_copy = jnp.einsum(
        "secf,edf->secd", grad_both, gate_up, preferred_element_type=jnp.float32
    ).astype(jnp.bfloat16)
    part_moe = jnp.einsum(
        "sect,secd->std", picks, grad_copy, preferred_element_type=jnp.float32
    ).astype(jnp.bfloat16)
    part_gates = jnp.sum(jnp.where(picks_wide, grad_slots[..., None], 0.0), axis=2)
    part_gates = lax.dynamic_update_slice_in_dim(
        jnp.zeros((dp_size, tok_dev, 128), jnp.float32), part_gates.transpose(0, 2, 1), first, 2
    )
    moe_sum, grad_gates = cube_scatter([part_moe, part_gates], "dp", 5)
    (out_sum,) = cube_scatter([part_out], "dp", 6)
    block_out = (hidden + out_sum).astype(jnp.bfloat16)
    grad_gates = grad_gates[:, :EXPERTS]
    grad_top = grad_out.astype(jnp.float32)
    grad_logits = gates * (grad_gates - jnp.sum(gates * grad_gates, axis=1, keepdims=True))
    router_wide = w_router.astype(jnp.float32)
    grad_moe = moe_sum + jnp.einsum("te,de->td", grad_logits, router_wide, precision=HIGH)
    grad_router = jnp.einsum("td,te->ed", moe_low.astype(jnp.float32), grad_logits, precision=HIGH)
    unused, moe_pull = jax.vjp(rms_scale, hidden, moe_gain)
    grad_hidden, grad_moe_gain = moe_pull(grad_moe)
    grad_hidden = grad_hidden + grad_top
    grad_hidden_low = grad_hidden.astype(jnp.bfloat16)
    grad_full = line_gather(grad_hidden_low, "mp", 7).reshape(row_count, D)
    grad_heads = jnp.dot(grad_full, out_part, preferred_element_type=jnp.float32).astype(
        jnp.bfloat16
    )
    grad_out_w = jnp.einsum("rd,rh->dh", grad_full, heads_low, preferred_element_type=jnp.float32)
    grad_query, grad_key, grad_value = lax.map(
        attend_backward,
        (
            grad_heads.reshape(seqs_here, length, head_local * HD),
            query_rot,
            key_rot,
            value_low,
            log_total,
            segments,
        ),
    )
    grad_qkv = jnp.concatenate(
        [
            grad_query.reshape(row_count, q_cols),
            grad_key.reshape(row_count, k_cols),
            grad_value.reshape(row_count, k_cols),
        ],
        axis=1,
    )
    grad_normed = line_scatter(
        jnp.einsum("rh,dh->rd", grad_qkv, qkv_full, preferred_element_type=jnp.float32)
        .astype(jnp.bfloat16)
        .reshape(-1, tok_dev, D),
        "mp",
        8,
    )
    unused_two, attn_pull = jax.vjp(rms_scale, own_rows, attn_gain)
    grad_own, grad_attn_gain = attn_pull(grad_normed)
    grad_in = grad_own + grad_hidden
    grad_qkv_w = jnp.einsum("rd,rh->dh", normed_low, grad_qkv, preferred_element_type=jnp.float32)
    grad_w = jnp.concatenate([grad_qkv_w, grad_out_w], axis=1).astype(jnp.bfloat16)
    (grad_w,) = cube_scatter([grad_w.reshape(dp_size, -1, grad_w.shape[1])], "dp", 9)
    small = jnp.concatenate(
        [
            grad_router,
            grad_attn_gain[None, :],
            grad_moe_gain[None, :],
            jnp.zeros((6, D), jnp.float32),
        ],
        axis=0,
    )
    small = total_of(small, ("dp", "mp"), 10)
    return (
        block_out,
        grad_in,
        small[EXPERTS],
        grad_w[:, :q_cols],
        grad_w[:, q_cols : q_cols + k_cols],
        grad_w[:, q_cols + k_cols : qkv_cols],
        grad_w[:, qkv_cols:],
        small[EXPERTS + 1],
        small[:EXPERTS].T,
        grad_gate_up,
        grad_down,
    )


def solution(mesh):
    placed = (
        P("dp", "mp"),
        P("dp", None),
        P(("dp", "mp"), None),
        P(),
        P("dp", "mp"),
        P("dp", "mp"),
        P("dp", "mp"),
        P("dp", "mp"),
        P(),
        P(),
        P("dp", None, "mp"),
        P("dp", None, "mp"),
        P(("dp", "mp"), None),
    )
    return jax.shard_map(
        local,
        mesh=mesh,
        in_specs=placed,
        out_specs=(
            P(("dp", "mp"), None),
            P(("dp", "mp"), None),
            P(),
            P("dp", "mp"),
            P("dp", "mp"),
            P("dp", "mp"),
            P("dp", "mp"),
            P(),
            P(),
            P("dp", None, "mp"),
            P("dp", None, "mp"),
        ),
        check_vma=False,
    )
```

time: 1220 us -> 905 us (0.74)
  waiting for transfers between devices: 790 us -> 1.42 us
  Pallas kernels: 0 us -> 621 us
  blocking collectives: 82.4 us -> 0 us
  other arithmetic: 98.1 us -> 53.4 us
  local copies, waits for them, and re-layouts: 63.5 us -> 42.4 us
  matrix products: 141 us -> 162 us
  starting transfers between devices: 20.6 us -> 0.16 us
    pallas_call x0 -> x10, Pallas kernels: none -> 621 us  [the longest x2 305 us: line_gather(): pl.pallas_call(functools.partial(line_gather_kernel, axis, size), out_sha...]
    reduce_scatter x6 -> x0, waiting for transfers between devices: 237 us -> none  [the longest x1 61.4 us: local(): lax.psum_scatter(jnp.einsum('rh,dh->rd', heads_low, out_part, preferred_e...]
    all_to_all x4 -> x0, waiting for transfers between devices: 168 us -> none  [the longest x1 61.7 us: local(): lax.all_to_all(grad_copy.reshape(dp_size, exp_dev * CAP, D), 'dp', split_...]
    all_gather x4 -> x2, waiting for transfers between devices: 159 us -> 0.01 us  [the longest x1 0.01 us: local(): gate_up = lax.all_gather(w_gate_up, 'mp', axis=2, tiled=True)]
    psum x1 -> x0, waiting for transfers between devices: 126 us -> none  [local(): lax.psum((grad_attn_gain, grad_moe_gain, grad_router), ('dp', 'mp'))]
    reduce_scatter x1, waiting for transfers between devices: 98.8 us -> 0.01 us  [local(): lax.psum_scatter(grad_gate_up.astype(jnp.bfloat16), 'mp', scatter_dimensi...]
    psum x1 -> x0, blocking collectives: 43.2 us -> none  [local(): lax.psum((grad_attn_gain, grad_moe_gain, grad_router), ('dp', 'mp'))]
    all_gather x4 -> x0, blocking collectives: 39.2 us -> none  [the longest x1 11 us: local(): lax.all_gather(w_key, 'dp', axis=0, tiled=True)]
  transfers between devices with their start and end apart: 17 -> 4, of which waited for: 15 -> 0; matrix products, arithmetic and copies ran while one was open for 17% -> 25% of each run, Pallas kernels for 0% -> 69%
where the time goes in v1:
time: 905 us; the launch traced here: 895 us
  Pallas kernels  621 us (69%)
  matrix products  162 us (18%)
  other arithmetic  53.4 us (6%)
  local copies, waits for them, and re-layouts  42.4 us (5%)
  between operations  15.1 us (2%)
    pallas_call x2, Pallas kernels, line_gather(): pl.pallas_call(functools.partial(line_gather_kernel, axis, size), out_sha...  305 us
    pallas_call x2, Pallas kernels, line_scatter(): pl.pallas_call(functools.partial(line_scatter_kernel, axis, size), out_sh...  133 us
    pallas_call x3, Pallas kernels, cube_scatter(): pl.pallas_call(functools.partial(scatter_kernel, axis, size, count), out_...  84.9 us
    pallas_call x2, Pallas kernels, cube_gather(): pl.pallas_call(functools.partial(gather_kernel, axis, size, count), out_s...  69.7 us
    pallas_call x1, Pallas kernels, total_of(): pl.pallas_call(functools.partial(total_kernel, sizes), out_shape=jax.Shap...  28.1 us
  transfers between devices with their start and end apart: 4, of which 0 were waited for; matrix products, arithmetic and copies ran while one was open for 25% of the time, Pallas kernels for 69%

profile of v1, /device:TPU:0, one launch (start us, length us, event | category | flops | bytes accessed | tf_op | source)
XLA Modules:
  0.0 895.2 jit_solution(3820995343788828962)
XLA Ops:
  8.7 160.2 %line_gather.2 = bf16[4,1024,256]{2,1,0:T(8,128)(2,1)} custom-call(bf16[1024,256]{1,0:T(8,128)(2,1)} %x_ref.1), custom_call_target="tpu_custom_call" | custom-call | bytes 80000000 | tf_op jit(solution)/shard_map/line_gather/pallas_call | solution.py:361
  169.0 2.1 convert_bitcast_fusion
  173.2 15.6 %cube_gather.2 = bf16[8,128,768]{2,1,0:T(8,128)(2,1)} custom-call(bf16[128,768]{1,0:T(8,128)(2,1)} %pad_maximum_fusion.7.refs_0_), custom_call_target="tpu_custom_call" | custom-call | bytes 60000000 | tf_op jit(solution)/shard_map/cube_gather/pallas_call | solution.py:210
  188.8 2.6 fusion.70
  195.5 7.4 fusion.96
  202.9 8.0 fusion.3
  210.9 8.2 fusion.57
  219.9 3.1 convolution_convert_fusion.1
  223.0 84.2 %line_scatter.2 = f32[256,1024]{1,0:T(8,128)} custom-call(bf16[4,256,1024]{2,1,0:T(8,128)(2,1)} %bitcast.196), custom_call_target="tpu_custom_call" | custom-call | bytes 80000000 | tf_op jit(solution)/shard_map/line_scatter/pallas_call | solution.py:438
  307.5 2.4 multiply_reduce_fusion.5
  311.7 54.1 %cube_gather.3 = (bf16[8,256,1024]{2,1,0:T(8,128)(2,1)}, bf16[8,256,1024]{2,1,0:T(8,128)(2,1)}, f32[8,256,128]{2,1,0:T(8,128)}) custom-call(bf16[256,1024]{1,0:T(8,128)(2,1)} %copy-done.8, bf16[256,1024]{1,0:T(8,128)(2,1)} %refs_1_.1, f32[256,128]{1,0:T(8,128)} %maximum_maximum_fusion.1.refs_2_), custom_call_target="tpu_custom_call" | custom-call | bytes 60000000 | tf_op jit(solution)/shard_map/cube_gather/pallas_call | solution.py:210
  365.8 2.2 dynamic-slice_bitcast_fusion
  368.6 6.6 fusion.43
  375.2 10.4 %fusion.28 = f32[8,4,96,1024]{3,2,0,1:T(8,128)S(1)} fusion(bf16[4,1024,1024]{2,1,0:T(8,128)(2,1)} %all-gather.3.cloned.1.call-done, bf16[8,4,96,1024]{3,2,1,0:T(8,128)(2,1)} %fusion.43), kind=kOutput, calls=%fused_computation.47 | convolution fusion | flops 6442450944 | bytes 27262976 | tf_op jit(solution)/shard_map/secd,edf->secf/dot_general | solution.py:594
  385.6 4.5 copy-done.5
  390.1 3.3 multiply_convert_fusion.1
  393.5 6.7 fusion.46
  400.2 5.9 fusion.6
  408.6 10.1 %bitcast_convert_fusion.1 = bf16[4,512,1024]{2,1,0:T(8,128)(2,1)} fusion(bf16[8,4,96,512]{3,2,0,1:T(8,128)(2,1)S(1)} %copy-done.19, f32[8,4,96,1024]{3,2,0,1:T(8,128)} %get-tuple-element.120, f32[8,4,96]{2,0,1:T(8,128)S(1)} %copy.108), kind=kOutput, calls=%fused_computation.20 | convolution fusion | flops 3229614080 | bytes 19935232 | tf_op jit(solution)/shard_map/secf,secd->efd/dot_general | solution.py:609
  418.9 13.9 %fusion.19 = (bf16[8,4,96,512]{3,2,0,1:T(8,128)(2,1)}, bf16[8,4,96,512]{3,2,0,1:T(8,128)(2,1)}) fusion(f32[8,4,96,1024]{3,2,0,1:T(8,128)} %copy-done.5, bf16[4,512,1024]{2,1,0:T(8,128)(2,1)} %all-gather.5.cloned.1.call-done, f32[8,4,96,1024]{3,2,0,1:T(8,128)} %get-tuple-element.120, f32[8,4,96]{2,0,1:T(8,128)S(1)} %copy.108), kind=kOutput, calls=%fused_computation.34 | convolution fusion | flops 3247964160 | bytes 35663872 | tf_op jit(solution)/shard_map/secd,efd->secf/dot_general | solution.py:606
  432.8 12.8 %bitcast_convert_fusion = bf16[4,1024,1024]{2,1,0:T(8,128)(2,1)} fusion(bf16[8,4,96,1024]{3,2,1,0:T(8,128)(2,1)} %fusion.43, bf16[8,4,96,512]{3,2,0,1:T(8,128)(2,1)} %get-tuple-element.92, bf16[8,4,96,512]{3,2,0,1:T(8,128)(2,1)} %get-tuple-element.91), kind=kOutput, calls=%fused_computation | convolution fusion | flops 6459228160 | bytes 20971520 | tf_op jit(solution)/shard_map/secd,secf->edf/dot_general | solution.py:619
  447.1 2.9 fusion.89
  450.0 2.6 copy.147
  454.6 5.9 dynamic_update_slice.24.refs_1_
  460.6 13.7 %fusion.11 = bf16[4,8,96,1024]{3,2,0,1:T(8,128)(2,1)} fusion(bf16[4,1024,1024]{2,1,0:T(8,128)(2,1)} %all-gather.3.cloned.1.call-done, bf16[8,4,96,512]{3,2,0,1:T(8,128)(2,1)} %get-tuple-element.92, bf16[8,4,96,512]{3,2,0,1:T(8,128)(2,1)} %get-tuple-element.91), kind=kOutput, calls=%fused_computation.23 | convolution fusion | flops 6455033856 | bytes 20971520 | tf_op jit(solution)/shard_map/secf,edf->secd/dot_general | solution.py:625
  474.3 7.3 bitcast_convert_fusion.2.refs_0_
  481.6 38.0 %cube_scatter.4 = (f32[256,1024]{1,0:T(8,128)}, f32[256,128]{1,0:T(8,128)}) custom-call(bf16[8,256,1024]{2,1,0:T(8,128)(2,1)} %bitcast_convert_fusion.2.refs_0_, f32[8,256,128]{2,1,0:T(8,128)} %copy-done.14), custom_call_target="tpu_custom_call" | custom-call | bytes 60000000 | tf_op jit(solution)/shard_map/cube_scatter/pallas_call | solution.py:282
  520.6 2.3 multiply_reduce_fusion
  524.1 145.1 %line_gather.3 = bf16[4,256,1024]{2,1,0:T(8,128)(2,1)} custom-call(bf16[256,1024]{1,0:T(8,128)(2,1)} %fusion.90.x_ref), custom_call_target="tpu_custom_call" | custom-call | bytes 80000000 | tf_op jit(solution)/shard_map/line_gather/pallas_call | solution.py:361
  669.1 2.4 convolution_convert_fusion.4
  671.6 15.2 %fusion = (f32[2,2,1024]{2,1,0:T(2,128)S(1)}, f32[2,1024,1024,2]{2,1,3,0:T(8,128)}) fusion(f32[2,2,1024,1024]{2,3,1,0:T(8,128)} %get-tuple-element.117, f32[2,2,1024]{2,1,0:T(2,128)S(1)} %log_add_fusion, bf16[1024,2,64,1]{0,2,3,1:T(8,128)(2,1)S(1)} %bitcast.214, bf16[1024,2,2,64]{0,3,2,1:T(8,128)(2,1)S(1)} %bitcast.206), kind=kOutput, calls=%fused_computation.3 | convolution fusion | flops 549449728 | bytes 34373632 | tf_op jit(solution)/shard_map/while/body/eval_jaxpr/qkgd,skd->kgqs/dot_general | solution.py:106
  688.3 8.3 fusion.2
  700.9 2.5 copy.119
  704.8 6.2 broadcast_multiply_fusion
  711.9 1.8 copy.122
  713.7 9.1 %fusion.61 = bf16[2,64,1024]{2,1,0:T(8,128)(2,1)} fusion(bf16[1024,2,2,64]{0,3,2,1:T(8,128)(2,1)S(1)} %bitcast.207, f32[2,2,1024,1024]{2,3,1,0:T(8,128)} %get-tuple-element.117, f32[2,2,1024]{2,1,0:T(2,128)S(1)} %log_add_fusion), kind=kOutput, calls=%fused_computation.82 | convolution fusion | flops 545390592 | bytes 17580032 | tf_op jit(solution)/shard_map/while/body/eval_jaxpr/kgqs,qkgd->skd/dot_general | solution.py:100
  722.8 1.9 copy.123
  724.7 4.1 copy.125
  728.8 2.6 convolution_convert_fusion.3
  736.4 15.6 %cube_scatter.5 = f32[128,768]{1,0:T(8,128)} custom-call(bf16[8,128,768]{2,1,0:T(8,128)(2,1)} %pad_maximum_fusion.1.refs_0_), custom_call_target="tpu_custom_call" | custom-call | bytes 60000000 | tf_op jit(solution)/shard_map/cube_scatter/pallas_call | solution.py:282
  752.1 4.2 convolution_convert_fusion
  756.3 48.4 %line_scatter.3 = f32[256,1024]{1,0:T(8,128)} custom-call(bf16[4,256,1024]{2,1,0:T(8,128)(2,1)} %bitcast.208), custom_call_target="tpu_custom_call" | custom-call | bytes 80000000 | tf_op jit(solution)/shard_map/line_scatter/pallas_call | solution.py:438
  807.5 28.1 %total.1 = f32[40,1024]{1,0:T(8,128)} custom-call(f32[40,1024]{1,0:T(8,128)} %maximum_maximum_fusion.x_ref), custom_call_target="tpu_custom_call" | custom-call | bytes 60000000 | tf_op jit(solution)/shard_map/total/pallas_call | solution.py:485
  835.6 7.4 bitcast_convert_fusion.3.refs_0_
  843.1 31.3 %cube_scatter.3 = f32[256,1024]{1,0:T(8,128)} custom-call(bf16[8,256,1024]{2,1,0:T(8,128)(2,1)} %bitcast_convert_fusion.3.refs_0_), custom_call_target="tpu_custom_call" | custom-call | bytes 60000000 | tf_op jit(solution)/shard_map/cube_scatter/pallas_call | solution.py:282
  878.9 2.9 fusion.65
  881.8 2.7 convert_element_type.225
  884.5 4.0 convert_element_type.223
  (196 shorter events, 39.1 us)
Async XLA Ops:
  7.2 302.8 %copy-start = (bf16[1024,32]{0,1:T(8,128)(2,1)S(1)}, bf16[1024,32]{0,1:T(8,128)(2,1)}, u32[]{:S(2)}) copy-start(bf16[1024,32]{0,1:T(8,128)(2,1)} %param.22) | copy-start | bytes 196612
  7.2 368.0 %all-gather.3.cloned.1.call-start = ((), (), s32[]{:S(2)}) async-start(), calls=%async_computation.2 | async-start | bytes 10485760 | tf_op jit(solution)/shard_map/all_gather | solution.py:519
  7.9 385.6 %all-gather.5.cloned.1.call-start = ((), (), s32[]{:S(2)}) async-start(), calls=%async_computation.3 | async-start | bytes 5242880 | tf_op jit(solution)/shard_map/all_gather | solution.py:520
  8.7 873.1 %reduce-scatter.5.cloned.1.call-start = ((), (), s32[]{:S(2)}) async-start(), calls=%async_computation.5 | async-start | bytes 5242880 | tf_op jit(solution)/shard_map/reduce_scatter | solution.py:612
  171.2 17.6 %copy-start.35 = (f32[1024]{0:T(1024)S(1)}, f32[1024]{0:T(1024)}, u32[]{:S(2)}) copy-start(f32[1024]{0:T(1024)} %param.16) | copy-start | bytes 12292
  172.4 19.2 %copy-start.2 = (f32[4,128,8,256]{3,2,0,1:T(8,128)}, f32[4,128,8,256]{3,2,0,1:T(8,128)S(1)}, u32[]{:S(2)}) copy-start(f32[4,128,8,256]{3,2,0,1:T(8,128)S(1)} %copy.149) | copy-start | bytes 12582916
  191.7 19.2 %copy-start.25 = (bf16[1024,128]{0,1:T(8,128)(2,1)}, bf16[1024,128]{0,1:T(8,128)(2,1)S(1)}, u32[]{:S(2)}) copy-start(bf16[1024,128]{0,1:T(8,128)(2,1)S(1)} %slice.168) | copy-start | bytes 786436
  195.2 7.7 copy-start.27
  195.5 7.4 copy-start.23
  202.9 8.0 copy-start.40
  210.9 8.2 copy-start.42
  219.1 88.1 %copy-start.53 = (s32[256,8]{0,1:T(8,128)S(1)}, s32[256,8]{0,1:T(8,128)}, u32[]{:S(2)}) copy-start(s32[256,8]{0,1:T(8,128)} %param.15) | copy-start | bytes 24580
  219.1 90.7 %copy-start.36 = (f32[1024]{0:T(1024)S(1)}, f32[1024]{0:T(1024)}, u32[]{:S(2)}) copy-start(f32[1024]{0:T(1024)} %param.21) | copy-start | bytes 12292
  309.8 58.1 %copy-start.49 = (f32[256]{0:T(256)}, f32[256]{0:T(256)S(1)}, u32[]{:S(2)}) copy-start(f32[256]{0:T(256)S(1)} %get-tuple-element.89) | copy-start | bytes 3076
  310.9 54.8 %copy-start.17 = (f32[256,32]{1,0:T(8,128)}, f32[256,32]{1,0:T(8,128)S(1)}, u32[]{:S(2)}) copy-start(f32[256,32]{1,0:T(8,128)S(1)} %fusion.80) | copy-start | bytes 98308
  393.5 6.7 copy-start.12
  400.2 7.0 copy-start.7
  400.2 8.4 copy-start.19
  408.6 10.2 %copy-start.46 = (f32[8,4,96]{2,0,1:T(8,128)}, f32[8,4,96]{2,0,1:T(8,128)S(1)}, u32[]{:S(2)}) copy-start(f32[8,4,96]{2,0,1:T(8,128)S(1)} %copy.108) | copy-start | bytes 36868
  418.8 465.7 %reduce-scatter.3.cloned.1.call-start = ((), (), s32[]{:S(2)}) async-start(), calls=%async_computation.4 | async-start | bytes 10485760 | tf_op jit(solution)/shard_map/reduce_scatter | solution.py:622
  445.8 7.4 copy-start.41
  445.8 7.4 copy-start.43
  460.5 13.8 %copy-start.14 = (f32[8,256,128]{2,1,0:T(8,128)}, f32[8,256,128]{2,1,0:T(8,128)S(1)}, u32[]{:S(2)}) copy-start(f32[8,256,128]{2,1,0:T(8,128)S(1)} %dynamic_update_slice.24.refs_1_) | copy-start | bytes 3145732
  474.3 45.3 %copy-start.18 = (f32[256,32]{1,0:T(8,128)S(1)}, f32[256,32]{1,0:T(8,128)}, u32[]{:S(2)}) copy-start(f32[256,32]{1,0:T(8,128)} %copy-done.17) | copy-start | bytes 98308
  481.6 41.3 %copy-start.48 = (f32[256]{0:T(256)S(1)}, f32[256]{0:T(256)}, u32[]{:S(2)}) copy-start(f32[256]{0:T(256)} %get-tuple-element.93) | copy-start | bytes 3076
  481.6 41.3 %copy-start.50 = (f32[256]{0:T(256)S(1)}, f32[256]{0:T(256)}, u32[]{:S(2)}) copy-start(f32[256]{0:T(256)} %copy-done.49) | copy-start | bytes 3076
  481.6 41.3 %copy-start.10 = (bf16[256,1024]{1,0:T(8,128)(2,1)S(1)}, bf16[256,1024]{1,0:T(8,128)(2,1)}, u32[]{:S(2)}) copy-start(bf16[256,1024]{1,0:T(8,128)(2,1)} %refs_1_.1) | copy-start | bytes 1572868
  520.6 150.9 %copy-start.51 = (f32[256]{0:T(256)}, f32[256]{0:T(256)S(1)}, u32[]{:S(2)}) copy-start(f32[256]{0:T(256)S(1)} %multiply_reduce_fusion.6) | copy-start | bytes 3076
  520.6 151.0 %copy-start.26 = (bf16[1024,128]{0,1:T(8,128)(2,1)S(1)}, bf16[1024,128]{0,1:T(8,128)(2,1)}, u32[]{:S(2)}) copy-start(bf16[1024,128]{0,1:T(8,128)(2,1)} %copy-done.25) | copy-start | bytes 786436
  671.6 15.2 %copy-start.20 = (bf16[1024,256]{0,1:T(8,128)(2,1)}, bf16[1024,256]{0,1:T(8,128)(2,1)S(1)}, u32[]{:S(2)}) copy-start(bf16[1024,256]{0,1:T(8,128)(2,1)S(1)} %convolution_convert_fusion.4) | copy-start | bytes 1572868
  671.6 15.2 %slice-start = ((s8[16777216]{0:T(1024)(128)(4,1)}), s8[4194304]{0:T(1024)(128)(4,1)S(1)}, s32[]{:S(2)}) async-start(s8[16777216]{0:T(1024)(128)(4,1)} %bitcast.184), calls=%async_computation.6 | async-start | bytes 8388608
  671.6 15.2 %slice-start.1 = ((s8[16777216]{0:T(1024)(128)(4,1)}), s8[4194304]{0:T(1024)(128)(4,1)S(1)}, s32[]{:S(2)}) async-start(s8[16777216]{0:T(1024)(128)(4,1)} %bitcast.184), calls=%async_computation.7 | async-start | bytes 8388608
  671.6 15.2 %slice-start.2 = ((s8[16777216]{0:T(1024)(128)(4,1)}), s8[4194304]{0:T(1024)(128)(4,1)S(1)}, s32[]{:S(2)}) async-start(s8[16777216]{0:T(1024)(128)(4,1)} %bitcast.184), calls=%async_computation.8 | async-start | bytes 8388608
  671.6 16.7 %slice-start.3 = ((s8[16777216]{0:T(1024)(128)(4,1)}), s8[4194304]{0:T(1024)(128)(4,1)S(1)}, s32[]{:S(2)}) async-start(s8[16777216]{0:T(1024)(128)(4,1)} %bitcast.184), calls=%async_computation.9 | async-start | bytes 8388608
  688.3 8.3 copy-start.28
  704.8 6.3 copy-start.29
  704.8 8.9 copy-start.21
  722.8 8.6 copy-start.13
  728.8 5.1 copy-start.22
  736.4 68.3 %copy-start.3 = (f32[4,128,8,256]{3,2,0,1:T(8,128)S(1)}, f32[4,128,8,256]{3,2,0,1:T(8,128)}, u32[]{:S(2)}) copy-start(f32[4,128,8,256]{3,2,0,1:T(8,128)} %copy-done.2) | copy-start | bytes 12582916
  752.0 54.2 %copy-start.9 = (bf16[256,1024]{1,0:T(8,128)(2,1)S(1)}, bf16[256,1024]{1,0:T(8,128)(2,1)}, u32[]{:S(2)}) copy-start(bf16[256,1024]{1,0:T(8,128)(2,1)} %copy-done.8) | copy-start | bytes 1572868
  752.0 54.2 %copy-start.24 = (f32[256,128]{1,0:T(8,128)S(1)}, f32[256,128]{1,0:T(8,128)}, u32[]{:S(2)}) copy-start(f32[256,128]{1,0:T(8,128)} %get-tuple-element.80) | copy-start | bytes 393220
  752.0 54.2 %copy-start.52 = (f32[256]{0:T(256)S(1)}, f32[256]{0:T(256)}, u32[]{:S(2)}) copy-start(f32[256]{0:T(256)} %copy-done.51) | copy-start | bytes 3076
  752.1 54.7 %copy-start.54 = (f32[40]{0:T(128)S(1)}, f32[40]{0:T(128)}, u32[]{:S(2)}) copy-start(f32[40]{0:T(128)} %pad.5.clone) | copy-start | bytes 484
  752.1 83.6 %copy-start.47 = (f32[8,4,96]{2,0,1:T(8,128)S(1)}, f32[8,4,96]{2,0,1:T(8,128)}, u32[]{:S(2)}) copy-start(f32[8,4,96]{2,0,1:T(8,128)} %copy-done.46) | copy-start | bytes 36868
  835.6 38.8 %copy-start.30 = (f32[40,1024]{1,0:T(8,128)S(1)}, f32[40,1024]{1,0:T(8,128)}, u32[]{:S(2)}) copy-start(f32[40,1024]{1,0:T(8,128)} %total.1) | copy-start | bytes 491524
  843.1 35.8 %copy-start.6 = (f32[256,1024]{1,0:T(8,128)S(1)}, f32[256,1024]{1,0:T(8,128)}, u32[]{:S(2)}) copy-start(f32[256,1024]{1,0:T(8,128)} %line_scatter.3) | copy-start | bytes 3145732
  843.1 35.8 %copy-start.11 = (bf16[256,1024]{1,0:T(8,128)(2,1)S(1)}, bf16[256,1024]{1,0:T(8,128)(2,1)}, u32[]{:S(2)}) copy-start(bf16[256,1024]{1,0:T(8,128)(2,1)} %refs_1_.1) | copy-start | bytes 1572868
  (15 other events, 33.5 us)
Sparse Core Ops, SparseCore 0:
  9.6 193.8 all-gather.2
  205.0 123.9 all-gather.4
  418.9 99.0 reduce-scatter.4
  520.3 178.3 reduce-scatter.2

commit v2 on v1

--- a/solution.py
+++ b/solution.py
@@ -516,9 +516,10 @@
     tok_dev = routes.shape[0]
     seqs_here = segments.shape[0]
     exp_dev = EXPERTS // dp_size
+    stacked = line_gather(block_in, "mp", 1)
+    stacked, w_gate_up, w_down = lax.optimization_barrier((stacked, w_gate_up, w_down))
     gate_up = lax.all_gather(w_gate_up, "mp", axis=2, tiled=True)
     down_full = lax.all_gather(w_down, "mp", axis=2, tiled=True)
-    stacked = line_gather(block_in, "mp", 1)
     full_rows = stacked.transpose(1, 0, 2).reshape(block_in.shape[0], -1)
     row_count = full_rows.shape[0]
     length = row_count // seqs_here
@@ -619,9 +620,6 @@
     grad_gate_up = jnp.einsum(
         "secd,secf->edf", arrived, grad_both, preferred_element_type=jnp.float32
     )
-    grad_gate_up = lax.psum_scatter(
-        grad_gate_up.astype(jnp.bfloat16), "mp", scatter_dimension=2, tiled=True
-    ).astype(jnp.float32)
     grad_copy = jnp.einsum(
         "secf,edf->secd", grad_both, gate_up, preferred_element_type=jnp.float32
     ).astype(jnp.bfloat16)
@@ -645,7 +643,14 @@
     grad_hidden, grad_moe_gain = moe_pull(grad_moe)
     grad_hidden = grad_hidden + grad_top
     grad_hidden_low = grad_hidden.astype(jnp.bfloat16)
-    grad_full = line_gather(grad_hidden_low, "mp", 7).reshape(row_count, D)
+    grad_full = line_gather(grad_hidden_low, "mp", 7)
+    grad_full, grad_gate_up = lax.optimization_barrier(
+        (grad_full, grad_gate_up.astype(jnp.bfloat16))
+    )
+    grad_full = grad_full.reshape(row_count, D)
+    grad_gate_up = lax.psum_scatter(
+        grad_gate_up, "mp", scatter_dimension=2, tiled=True
+    ).astype(jnp.float32)
     grad_heads = jnp.dot(grad_full, out_part, preferred_element_type=jnp.float32).astype(
         jnp.bfloat16
     )

time: 905 us -> 763 us (0.84)
  Pallas kernels: 621 us -> 431 us
  waiting for transfers between devices: 1.42 us -> 37.4 us
    pallas_call x2, Pallas kernels: 305 us -> 80.8 us  [line_gather(): pl.pallas_call(functools.partial(line_gather_kernel, axis, size), out_sha...]
    all_gather x1, waiting for transfers between devices: 0.01 us -> 36.6 us  [local(): down_full = lax.all_gather(w_down, 'mp', axis=2, tiled=True)]
    pallas_call x2, Pallas kernels: 133 us -> 168 us  [line_scatter(): pl.pallas_call(functools.partial(line_scatter_kernel, axis, size), out_sh...]
  transfers between devices with their start and end apart: 4 -> 4, of which waited for: 0 -> 1; matrix products, arithmetic and copies ran while one was open for 25% -> 31% of each run, Pallas kernels for 69% -> 52%
where the time goes in v2:
time: 763 us; the launch traced here: 753 us
  Pallas kernels  431 us (56%)
  matrix products  170 us (22%)
  other arithmetic  58.4 us (8%)
  local copies, waits for them, and re-layouts  40.7 us (5%)
  waiting for transfers between devices  37.4 us (5%)
  between operations  15 us (2%)
    pallas_call x2, Pallas kernels, line_scatter(): pl.pallas_call(functools.partial(line_scatter_kernel, axis, size), out_sh...  168 us
    pallas_call x3, Pallas kernels, cube_scatter(): pl.pallas_call(functools.partial(scatter_kernel, axis, size, count), out_...  83.9 us
    pallas_call x2, Pallas kernels, line_gather(): pl.pallas_call(functools.partial(line_gather_kernel, axis, size), out_sha...  80.8 us
    pallas_call x2, Pallas kernels, cube_gather(): pl.pallas_call(functools.partial(gather_kernel, axis, size, count), out_s...  71.8 us
    all_gather x1, waiting for transfers between devices, local(): down_full = lax.all_gather(w_down, 'mp', axis=2, tiled=True)  36.6 us
    pallas_call x1, Pallas kernels, total_of(): pl.pallas_call(functools.partial(total_kernel, sizes), out_shape=jax.Shap...  26.9 us
  transfers between devices with their start and end apart: 4, of which 1 were waited for; matrix products, arithmetic and copies ran while one was open for 31% of the time, Pallas kernels for 52%

profile of v2, /device:TPU:0, one launch (start us, length us, event | category | flops | bytes accessed | tf_op | source)
XLA Modules:
  0.0 753.0 jit_solution(16334278060659507353)
XLA Ops:
  7.2 42.6 %line_gather.2 = bf16[4,1024,256]{2,1,0:T(8,128)(2,1)} custom-call(bf16[1024,256]{1,0:T(8,128)(2,1)} %x_ref.1), custom_call_target="tpu_custom_call" | custom-call | bytes 80000000 | tf_op jit(solution)/shard_map/line_gather/pallas_call | solution.py:361
  50.7 2.0 convert_bitcast_fusion
  54.8 15.5 %cube_gather.2 = bf16[8,128,768]{2,1,0:T(8,128)(2,1)} custom-call(bf16[128,768]{1,0:T(8,128)(2,1)} %pad_maximum_fusion.7.refs_0_), custom_call_target="tpu_custom_call" | custom-call | bytes 60000000 | tf_op jit(solution)/shard_map/cube_gather/pallas_call | solution.py:210
  70.3 2.7 fusion.70
  77.0 7.4 fusion.96
  84.3 8.1 %fusion.3 = f32[2,2,1024]{2,1,0:T(2,128)S(1)} fusion(f32[2,2,1024,1024]{2,3,1,0:T(8,128)} %get-tuple-element.127, f32[2,2,1024]{2,1,0:T(2,128)S(1)} %get-tuple-element.126), kind=kLoop, calls=%fused_computation.10 | loop fusion | flops 8384512 | bytes 16809984 | tf_op jit(solution)/shard_map/while/body/eval_jaxpr/reduce_sum | solution.py:75
  92.5 7.5 fusion.57
  100.8 3.1 convolution_convert_fusion.1
  103.9 86.6 %line_scatter.2 = f32[256,1024]{1,0:T(8,128)} custom-call(bf16[4,256,1024]{2,1,0:T(8,128)(2,1)} %bitcast.196), custom_call_target="tpu_custom_call" | custom-call | bytes 80000000 | tf_op jit(solution)/shard_map/line_scatter/pallas_call | solution.py:438
  194.4 56.3 %cube_gather.3 = (bf16[8,256,1024]{2,1,0:T(8,128)(2,1)}, bf16[8,256,1024]{2,1,0:T(8,128)(2,1)}, f32[8,256,128]{2,1,0:T(8,128)}) custom-call(bf16[256,1024]{1,0:T(8,128)(2,1)} %copy-done.7, bf16[256,1024]{1,0:T(8,128)(2,1)} %refs_1_.1, f32[256,128]{1,0:T(8,128)} %maximum_maximum_fusion.1.refs_2_), custom_call_target="tpu_custom_call" | custom-call | bytes 60000000 | tf_op jit(solution)/shard_map/cube_gather/pallas_call | solution.py:210
  250.7 2.2 dynamic-slice_bitcast_fusion
  253.6 6.6 fusion.43
  260.1 14.0 %fusion.28 = f32[8,4,96,1024]{3,2,0,1:T(8,128)} fusion(bf16[8,4,96,1024]{3,2,1,0:T(8,128)(2,1)} %fusion.43, bf16[4,1024,1024]{2,1,0:T(8,128)(2,1)} %all-gather.5.cloned.1.call-done), kind=kOutput, calls=%fused_computation.47 | convolution fusion | flops 6442450944 | bytes 27262976 | tf_op jit(solution)/shard_map/secd,edf->secf/dot_general | solution.py:595
  274.2 6.9 multiply_convert_fusion.1
  281.1 36.6 %all-gather.3.cloned.1.call-done = bf16[4,512,1024]{2,1,0:T(8,128)(2,1)} async-done(((bf16[4,512,256]{2,1,0:T(8,128)(2,1)}), bf16[4,512,1024]{2,1,0:T(8,128)(2,1)}) %all-gather.3.cloned.1.call-update) | async-done | bytes 4194320 | tf_op jit(solution)/shard_map/all_gather | solution.py:522
  317.7 6.6 fusion.46
  324.3 10.5 %fusion.6 = (f32[8,4,96]{2,0,1:T(8,128)S(1)}, f32[8,4,96,1024]{3,2,0,1:T(8,128)}) fusion(bf16[4,1024,8,96]{1,3,2,0:T(8,128)(2,1)S(1)} %fusion.46, bf16[8,256,1024]{2,1,0:T(8,128)(2,1)} %get-tuple-element.86, f32[8,4,256]{2,1,0:T(4,128)S(1)} %copy.106), kind=kOutput, calls=%fused_computation.15 | convolution fusion | flops 1620833280 | bytes 23113728 | tf_op jit(solution)/shard_map/sect,std->secd/dot_general | solution.py:593
  336.3 11.0 %bitcast_convert_fusion.1 = bf16[4,512,1024]{2,1,0:T(8,128)(2,1)} fusion(bf16[8,4,96,512]{3,2,0,1:T(8,128)(2,1)} %multiply_convert_fusion.1, f32[8,4,96,1024]{3,2,0,1:T(8,128)} %get-tuple-element.130, f32[8,4,96]{2,0,1:T(8,128)S(1)} %copy.108), kind=kOutput, calls=%fused_computation.20 | convolution fusion | flops 3229614080 | bytes 19935232 | tf_op jit(solution)/shard_map/secf,secd->efd/dot_general | solution.py:610
  348.8 6.0 dynamic_update_slice.24.refs_1_
  354.8 14.4 %fusion.19 = (bf16[8,4,96,512]{3,2,0,1:T(8,128)(2,1)}, bf16[8,4,96,512]{3,2,0,1:T(8,128)(2,1)}) fusion(f32[8,4,96,1024]{3,2,0,1:T(8,128)} %fusion.28, f32[8,4,96,1024]{3,2,0,1:T(8,128)} %get-tuple-element.130, f32[8,4,96]{2,0,1:T(8,128)S(1)} %copy.108, bf16[4,512,1024]{2,1,0:T(8,128)(2,1)} %all-gather.3.cloned.1.call-done), kind=kOutput, calls=%fused_computation.34 | convolution fusion | flops 3247964160 | bytes 35663872 | tf_op jit(solution)/shard_map/secd,efd->secf/dot_general | solution.py:607
  369.2 13.0 %fusion.11 = bf16[4,1024,8,96]{1,3,0,2:T(8,128)(2,1)} fusion(bf16[4,1024,1024]{2,1,0:T(8,128)(2,1)} %all-gather.5.cloned.1.call-done, bf16[8,4,96,512]{3,2,0,1:T(8,128)(2,1)} %get-tuple-element.102, bf16[8,4,96,512]{3,2,0,1:T(8,128)(2,1)} %get-tuple-element.101), kind=kOutput, calls=%fused_computation.23 | convolution fusion | flops 6455033856 | bytes 20971520 | tf_op jit(solution)/shard_map/secf,edf->secd/dot_general | solution.py:623
  382.2 7.2 bitcast_convert_fusion.2.refs_0_
  389.4 37.6 %cube_scatter.4 = (f32[256,1024]{1,0:T(8,128)}, f32[256,128]{1,0:T(8,128)}) custom-call(bf16[8,256,1024]{2,1,0:T(8,128)(2,1)} %bitcast_convert_fusion.2.refs_0_, f32[8,256,128]{2,1,0:T(8,128)} %copy-done.12), custom_call_target="tpu_custom_call" | custom-call | bytes 60000000 | tf_op jit(solution)/shard_map/cube_scatter/pallas_call | solution.py:282
  428.0 2.2 multiply_reduce_fusion
  431.4 38.2 %line_gather.3 = bf16[4,256,1024]{2,1,0:T(8,128)(2,1)} custom-call(bf16[256,1024]{1,0:T(8,128)(2,1)} %fusion.90.x_ref), custom_call_target="tpu_custom_call" | custom-call | bytes 80000000 | tf_op jit(solution)/shard_map/line_gather/pallas_call | solution.py:361
  469.6 12.4 %bitcast_convert_fusion = bf16[4,1024,1024]{2,1,0:T(8,128)(2,1)} fusion(bf16[8,4,96,1024]{3,2,1,0:T(8,128)(2,1)} %fusion.43, bf16[8,4,96,512]{3,2,0,1:T(8,128)(2,1)} %get-tuple-element.102, bf16[8,4,96,512]{3,2,0,1:T(8,128)(2,1)S(1)} %copy-done.49), kind=kOutput, calls=%fused_computation.5 | convolution fusion | flops 6459228160 | bytes 20971520 | tf_op jit(solution)/shard_map/secd,secf->edf/dot_general | solution.py:620
  484.1 2.5 copy.119
  486.7 4.5 fusion.89
  491.1 3.9 copy.147
  495.1 2.5 convolution_convert_fusion.4
  497.7 15.1 %fusion = (f32[2,2,1024]{2,1,0:T(2,128)S(1)}, f32[2,1024,1024,2]{2,1,3,0:T(8,128)}) fusion(f32[2,2,1024,1024]{2,3,1,0:T(8,128)} %get-tuple-element.127, f32[2,2,1024]{2,1,0:T(2,128)S(1)} %log_add_fusion, bf16[1024,2,64,1]{0,2,3,1:T(8,128)(2,1)S(1)} %bitcast.214, bf16[1024,2,2,64]{0,3,2,1:T(8,128)(2,1)S(1)} %bitcast.206), kind=kOutput, calls=%fused_computation.2 | convolution fusion | flops 549449728 | bytes 34373632 | tf_op jit(solution)/shard_map/while/body/eval_jaxpr/qkgd,skd->kgqs/dot_general | solution.py:106
  514.4 8.5 %fusion.2 = bf16[2,2,1024,1024]{2,3,1,0:T(8,128)(2,1)S(1)} fusion(f32[2,1024,1024,2]{2,1,3,0:T(8,128)} %get-tuple-element.133, f32[2,2,1024,1024]{2,3,1,0:T(8,128)S(1)} %bitcast.185, f32[2,2,1024]{2,1,0:T(2,128)S(1)} %get-tuple-element.132, f32[2,2,1024]{2,1,0:T(2,128)S(1)} %log_add_fusion), kind=kLoop, calls=%fused_computation.4 | loop fusion | flops 16777216 | bytes 41975808 | tf_op jit(solution)/shard_map/while/body/eval_jaxpr/convert_element_type | solution.py:110
  527.2 2.6 copy.120
  531.1 6.3 broadcast_multiply_fusion
  540.0 9.4 %fusion.61 = bf16[2,64,1024]{2,1,0:T(8,128)(2,1)} fusion(bf16[1024,2,2,64]{0,3,2,1:T(8,128)(2,1)S(1)} %bitcast.207, f32[2,2,1024,1024]{2,3,1,0:T(8,128)} %get-tuple-element.127, f32[2,2,1024]{2,1,0:T(2,128)S(1)} %log_add_fusion), kind=kOutput, calls=%fused_computation.82 | convolution fusion | flops 545390592 | bytes 17580032 | tf_op jit(solution)/shard_map/while/body/eval_jaxpr/kgqs,qkgd->skd/dot_general | solution.py:100
  549.5 1.9 copy.124
  551.3 4.0 copy.126
  555.3 2.6 convolution_convert_fusion.3
  557.9 1.8 add_convert_fusion
  563.0 16.9 %cube_scatter.5 = f32[128,768]{1,0:T(8,128)} custom-call(bf16[8,128,768]{2,1,0:T(8,128)(2,1)} %pad_maximum_fusion.1.refs_0_), custom_call_target="tpu_custom_call" | custom-call | bytes 60000000 | tf_op jit(solution)/shard_map/cube_scatter/pallas_call | solution.py:282
  579.9 4.2 convolution_convert_fusion
  584.1 81.4 %line_scatter.3 = f32[256,1024]{1,0:T(8,128)} custom-call(bf16[4,256,1024]{2,1,0:T(8,128)(2,1)} %bitcast.208), custom_call_target="tpu_custom_call" | custom-call | bytes 80000000 | tf_op jit(solution)/shard_map/line_scatter/pallas_call | solution.py:438
  668.3 26.9 %total.1 = f32[40,1024]{1,0:T(8,128)} custom-call(f32[40,1024]{1,0:T(8,128)} %maximum_maximum_fusion.x_ref), custom_call_target="tpu_custom_call" | custom-call | bytes 60000000 | tf_op jit(solution)/shard_map/total/pallas_call | solution.py:485
  695.3 7.4 bitcast_convert_fusion.3.refs_0_
  702.7 29.5 %cube_scatter.3 = f32[256,1024]{1,0:T(8,128)} custom-call(bf16[8,256,1024]{2,1,0:T(8,128)(2,1)} %bitcast_convert_fusion.3.refs_0_), custom_call_target="tpu_custom_call" | custom-call | bytes 60000000 | tf_op jit(solution)/shard_map/cube_scatter/pallas_call | solution.py:282
  736.7 2.9 fusion.65
  739.6 2.7 convert_element_type.225
  742.3 4.0 convert_element_type.223
  (186 shorter events, 39.4 us)
Async XLA Ops:
  7.2 185.6 %copy-start = (bf16[1024,32]{0,1:T(8,128)(2,1)S(1)}, bf16[1024,32]{0,1:T(8,128)(2,1)}, u32[]{:S(2)}) copy-start(bf16[1024,32]{0,1:T(8,128)(2,1)} %param.22) | copy-start | bytes 196612
  7.2 252.9 %all-gather.5.cloned.1.call-start = ((), (), s32[]{:S(2)}) async-start(), calls=%async_computation.3 | async-start | bytes 10485760 | tf_op jit(solution)/shard_map/all_gather | solution.py:521
  49.9 2.8 copy-start.4
  49.9 267.8 %all-gather.3.cloned.1.call-start = ((), (), s32[]{:S(2)}) async-start(), calls=%async_computation.2 | async-start | bytes 5242880 | tf_op jit(solution)/shard_map/all_gather | solution.py:522
  50.7 688.9 %reduce-scatter.5.cloned.1.call-start = ((), (), s32[]{:S(2)}) async-start(), calls=%async_computation.5 | async-start | bytes 5242880 | tf_op jit(solution)/shard_map/reduce_scatter | solution.py:613
  52.7 17.5 %copy-start.32 = (f32[1024]{0:T(1024)S(1)}, f32[1024]{0:T(1024)}, u32[]{:S(2)}) copy-start(f32[1024]{0:T(1024)} %param.16) | copy-start | bytes 12292
  53.9 19.2 %copy-start.2 = (f32[4,128,8,256]{3,2,0,1:T(8,128)}, f32[4,128,8,256]{3,2,0,1:T(8,128)S(1)}, u32[]{:S(2)}) copy-start(f32[4,128,8,256]{3,2,0,1:T(8,128)S(1)} %copy.149) | copy-start | bytes 12582916
  54.0 19.1 %copy-start.38 = (f32[1024]{0:T(1024)}, f32[1024]{0:T(1024)S(1)}, u32[]{:S(2)}) copy-start(f32[1024]{0:T(1024)S(1)} %add_rsqrt_fusion) | copy-start | bytes 12292
  70.3 3.0 copy-start.35
  73.1 19.3 %copy-start.22 = (bf16[1024,128]{0,1:T(8,128)(2,1)}, bf16[1024,128]{0,1:T(8,128)(2,1)S(1)}, u32[]{:S(2)}) copy-start(bf16[1024,128]{0,1:T(8,128)(2,1)S(1)} %slice.168) | copy-start | bytes 786436
  76.6 7.7 %copy-start.24 = (bf16[1024,2,64,1]{0,2,3,1:T(8,128)(2,1)}, bf16[1024,2,64,1]{0,2,3,1:T(8,128)(2,1)S(1)}, u32[]{:S(2)}) copy-start(bf16[1024,2,64,1]{0,2,3,1:T(8,128)(2,1)S(1)} %fusion.77) | copy-start | bytes 786436
  77.0 7.4 copy-start.20
  100.0 90.5 %copy-start.48 = (s32[256,8]{0,1:T(8,128)S(1)}, s32[256,8]{0,1:T(8,128)}, u32[]{:S(2)}) copy-start(s32[256,8]{0,1:T(8,128)} %param.15) | copy-start | bytes 24580
  100.0 92.6 %copy-start.34 = (f32[1024]{0:T(1024)S(1)}, f32[1024]{0:T(1024)}, u32[]{:S(2)}) copy-start(f32[1024]{0:T(1024)} %param.21) | copy-start | bytes 12292
  192.5 237.7 %copy-start.46 = (f32[256]{0:T(256)}, f32[256]{0:T(256)S(1)}, u32[]{:S(2)}) copy-start(f32[256]{0:T(256)S(1)} %get-tuple-element.103) | copy-start | bytes 3076
  192.8 1.7 copy-start.7
  324.3 10.6 %copy-start.6 = (bf16[4,1024,8,96]{1,3,2,0:T(8,128)(2,1)}, bf16[4,1024,8,96]{1,3,2,0:T(8,128)(2,1)S(1)}, u32[]{:S(2)}) copy-start(bf16[4,1024,8,96]{1,3,2,0:T(8,128)(2,1)S(1)} %fusion.46) | copy-start | bytes 18874372
  336.2 18.5 %copy-start.42 = (f32[8,4,96]{2,0,1:T(8,128)}, f32[8,4,96]{2,0,1:T(8,128)S(1)}, u32[]{:S(2)}) copy-start(f32[8,4,96]{2,0,1:T(8,128)S(1)} %copy.108) | copy-start | bytes 36868
  347.3 395.0 %reduce-scatter.3.cloned.1.call-start = ((), (), s32[]{:S(2)}) async-start(), calls=%async_computation.4 | async-start | bytes 10485760 | tf_op jit(solution)/shard_map/reduce_scatter | solution.py:651
  354.8 14.5 %copy-start.12 = (f32[8,256,128]{2,1,0:T(8,128)}, f32[8,256,128]{2,1,0:T(8,128)S(1)}, u32[]{:S(2)}) copy-start(f32[8,256,128]{2,1,0:T(8,128)S(1)} %dynamic_update_slice.24.refs_1_) | copy-start | bytes 3145732
  389.4 40.9 %copy-start.9 = (bf16[256,1024]{1,0:T(8,128)(2,1)S(1)}, bf16[256,1024]{1,0:T(8,128)(2,1)}, u32[]{:S(2)}) copy-start(bf16[256,1024]{1,0:T(8,128)(2,1)} %refs_1_.1) | copy-start | bytes 1572868
  389.4 80.2 %copy-start.49 = (bf16[8,4,96,512]{3,2,0,1:T(8,128)(2,1)S(1)}, bf16[8,4,96,512]{3,2,0,1:T(8,128)(2,1)}, u32[]{:S(2)}) copy-start(bf16[8,4,96,512]{3,2,0,1:T(8,128)(2,1)} %get-tuple-element.101) | copy-start | bytes 9437188
  430.3 235.3 %copy-start.44 = (f32[256]{0:T(256)}, f32[256]{0:T(256)S(1)}, u32[]{:S(2)}) copy-start(f32[256]{0:T(256)S(1)} %get-tuple-element.137) | copy-start | bytes 3076
  482.1 4.6 copy-start.33
  482.1 4.6 copy-start.39
  486.7 11.0 %copy-start.23 = (bf16[1024,128]{0,1:T(8,128)(2,1)S(1)}, bf16[1024,128]{0,1:T(8,128)(2,1)}, u32[]{:S(2)}) copy-start(bf16[1024,128]{0,1:T(8,128)(2,1)} %copy-done.22) | copy-start | bytes 786436
  497.6 15.2 %copy-start.17 = (bf16[1024,256]{0,1:T(8,128)(2,1)}, bf16[1024,256]{0,1:T(8,128)(2,1)S(1)}, u32[]{:S(2)}) copy-start(bf16[1024,256]{0,1:T(8,128)(2,1)S(1)} %convolution_convert_fusion.4) | copy-start | bytes 1572868
  497.6 15.2 %slice-start = ((s8[16777216]{0:T(1024)(128)(4,1)}), s8[4194304]{0:T(1024)(128)(4,1)S(1)}, s32[]{:S(2)}) async-start(s8[16777216]{0:T(1024)(128)(4,1)} %bitcast.184), calls=%async_computation.6 | async-start | bytes 8388608
  497.7 15.1 %slice-start.1 = ((s8[16777216]{0:T(1024)(128)(4,1)}), s8[4194304]{0:T(1024)(128)(4,1)S(1)}, s32[]{:S(2)}) async-start(s8[16777216]{0:T(1024)(128)(4,1)} %bitcast.184), calls=%async_computation.7 | async-start | bytes 8388608
  497.7 15.1 %slice-start.2 = ((s8[16777216]{0:T(1024)(128)(4,1)}), s8[4194304]{0:T(1024)(128)(4,1)S(1)}, s32[]{:S(2)}) async-start(s8[16777216]{0:T(1024)(128)(4,1)} %bitcast.184), calls=%async_computation.8 | async-start | bytes 8388608
  497.7 16.7 %slice-start.3 = ((s8[16777216]{0:T(1024)(128)(4,1)}), s8[4194304]{0:T(1024)(128)(4,1)S(1)}, s32[]{:S(2)}) async-start(s8[16777216]{0:T(1024)(128)(4,1)} %bitcast.184), calls=%async_computation.9 | async-start | bytes 8388608
  514.4 8.5 %copy-start.25 = (bf16[1024,2,64,1]{0,2,3,1:T(8,128)(2,1)S(1)}, bf16[1024,2,64,1]{0,2,3,1:T(8,128)(2,1)}, u32[]{:S(2)}) copy-start(bf16[1024,2,64,1]{0,2,3,1:T(8,128)(2,1)} %copy-done.24) | copy-start | bytes 786436
  522.9 3.2 copy-start.1
  531.1 6.4 copy-start.26
  531.1 9.0 %copy-start.18 = (bf16[1024,256]{0,1:T(8,128)(2,1)S(1)}, bf16[1024,256]{0,1:T(8,128)(2,1)}, u32[]{:S(2)}) copy-start(bf16[1024,256]{0,1:T(8,128)(2,1)} %copy-done.17) | copy-start | bytes 1572868
  549.4 8.4 %copy-start.11 = (f32[1024,256]{1,0:T(8,128)S(1)}, f32[1024,256]{1,0:T(8,128)}, u32[]{:S(2)}) copy-start(f32[1024,256]{1,0:T(8,128)} %copy.119) | copy-start | bytes 3145732
  555.3 5.2 copy-start.19
  555.3 5.2 copy-start.30
  555.3 5.2 copy-start.31
  563.0 102.6 %copy-start.3 = (f32[4,128,8,256]{3,2,0,1:T(8,128)S(1)}, f32[4,128,8,256]{3,2,0,1:T(8,128)}, u32[]{:S(2)}) copy-start(f32[4,128,8,256]{3,2,0,1:T(8,128)} %copy-done.2) | copy-start | bytes 12582916
  579.9 87.2 %copy-start.8 = (bf16[256,1024]{1,0:T(8,128)(2,1)S(1)}, bf16[256,1024]{1,0:T(8,128)(2,1)}, u32[]{:S(2)}) copy-start(bf16[256,1024]{1,0:T(8,128)(2,1)} %copy-done.7) | copy-start | bytes 1572868
  579.9 87.2 %copy-start.21 = (f32[256,128]{1,0:T(8,128)S(1)}, f32[256,128]{1,0:T(8,128)}, u32[]{:S(2)}) copy-start(f32[256,128]{1,0:T(8,128)} %get-tuple-element.88) | copy-start | bytes 393220
  579.9 115.3 %copy-start.43 = (f32[8,4,96]{2,0,1:T(8,128)S(1)}, f32[8,4,96]{2,0,1:T(8,128)}, u32[]{:S(2)}) copy-start(f32[8,4,96]{2,0,1:T(8,128)} %copy-done.42) | copy-start | bytes 36868
  695.3 36.9 %copy-start.47 = (f32[256]{0:T(256)S(1)}, f32[256]{0:T(256)}, u32[]{:S(2)}) copy-start(f32[256]{0:T(256)} %copy-done.46) | copy-start | bytes 3076
  695.3 36.9 %copy-start.27 = (f32[40,1024]{1,0:T(8,128)S(1)}, f32[40,1024]{1,0:T(8,128)}, u32[]{:S(2)}) copy-start(f32[40,1024]{1,0:T(8,128)} %total.1) | copy-start | bytes 491524
  702.7 34.0 %copy-start.5 = (f32[256,1024]{1,0:T(8,128)S(1)}, f32[256,1024]{1,0:T(8,128)}, u32[]{:S(2)}) copy-start(f32[256,1024]{1,0:T(8,128)} %line_scatter.3) | copy-start | bytes 3145732
  702.7 34.0 %copy-start.10 = (bf16[256,1024]{1,0:T(8,128)(2,1)S(1)}, bf16[256,1024]{1,0:T(8,128)(2,1)}, u32[]{:S(2)}) copy-start(bf16[256,1024]{1,0:T(8,128)(2,1)} %refs_1_.1) | copy-start | bytes 1572868
  702.7 34.0 %copy-start.45 = (f32[256]{0:T(256)S(1)}, f32[256]{0:T(256)}, u32[]{:S(2)}) copy-start(f32[256]{0:T(256)} %copy-done.44) | copy-start | bytes 3076
  (10 other events, 10.6 us)
Sparse Core Ops, SparseCore 0:
  50.0 183.1 all-gather.4
  234.8 82.8 all-gather.2
  347.4 74.9 reduce-scatter.4
  482.2 176.7 reduce-scatter.2
